TPU v7x, 128 devices: a whole 4x4x4 slice. The times are simulated.
128 devices in a mesh: row: 16 (over x, z), col: 8 (over y, core).
Axes of the slice: x: 4, y: 4, z: 4, core: 2. Of those that a mesh axis runs over, the one named last changes fastest.
Arguments:
- far_left: bfloat16 [16, 8, 128, 128, 256], P('row', 'col'), may hold values from -6.92749e-05 to 6.92749e-05
- far_right: bfloat16 [16, 8, 128, 128, 256], P('row', 'col'), may hold values from -0.47 to 0.47
- far_rank: int32 [16, 8, 128], P('row', 'col'), may hold values from 8 to 128, as said below
- near_tiles: bfloat16 [128, 3, 256, 256], P(('row', 'col')), may hold values from -0.0004108677 to 0.0004108677
- near_cols: int32 [128, 3], P(('row', 'col')), may hold values from 0 to 15, as said below
- data: float32 [16, 8, 256, 128], P('row', 'col'), may hold values from -40 to 40
- reg_weight: float32 [128], replicated, may hold values from 0.05 to 0.5
Outputs:
- solution: float32 [8, 16, 256, 128], P('col', 'row')
- misfit: float32 [16, 8, 256, 128], P('row', 'col')
- regularized: float32 [8, 16, 256, 128], P('col', 'row')
Inputs may be any that keep to these rules, and one draw needn't show every extreme that they name: `far_rank`: each leaf's rank is 128 divided by a power of two, at least 1; the first leaf of every device block has rank 128. `near_cols`: the 3 columns of a leaf row I are distinct and lie among five neighbouring leaf columns that contain I % 16 or touch the edge of the column block.
All inputs are finite; a program needn't handle non-finite values.
Results may differ from a plain program's by a relative error of at most 0.0085.
Values may be sent and summed in bfloat16 or wider, within the bound.
No kernel may reach another device: no remote copies, remote signals or barrier semaphores. Data moves between devices by JAX's collectives and lax.ppermute only.
A program may use at most 128 MiB of HBM per device.

v0:
```python
import jax
import jax.numpy as jnp
from jax import lax
from jax.experimental import pallas as pl
from jax.experimental.pallas import tpu as pltpu
from jax.sharding import PartitionSpec as P

F32 = jnp.float32
BF16 = jnp.bfloat16
ROWS = 16
COLS = 8
RANK = 128
RHS = 128
LEAF = 256
BAND = 3
EXTRA = 16
MSG = RHS + EXTRA
ORDER = (1, 3, 2)
SUMS = 24
FULL = 32000.0
VMEM = pl.BlockSpec(memory_space=pltpu.VMEM)
SMEM = pl.BlockSpec(memory_space=pltpu.SMEM)
HBM = pl.BlockSpec(memory_space=pl.ANY)


def shape(dims, dtype=F32):
    return jax.ShapeDtypeStruct(dims, dtype)


def call(kernel, outs, *args, specs=None, scratch=(), limit=8, flops=0):
    return pl.pallas_call(
        kernel,
        out_shape=outs,
        in_specs=specs or [VMEM] * len(args),
        out_specs=jax.tree.map(lambda _: VMEM, outs),
        scratch_shapes=list(scratch),
        compiler_params=pltpu.CompilerParams(vmem_limit_bytes=limit << 20),
        cost_estimate=pl.CostEstimate(flops=flops, bytes_accessed=1 << 16, transcendentals=0),
    )(*args)


def nt(left, right):
    return lax.dot_general(left, right, (((1,), (1,)), ((), ())), preferred_element_type=F32)


def nn(left, right):
    return jnp.dot(left, right, preferred_element_type=F32)


def row_sum(values):
    folded = values[:, :RHS] + values[:, RHS:]
    return jnp.sum(folded.T, axis=0, keepdims=True)


def as_column(row):
    square = jnp.broadcast_to(row, (RHS, RHS)).T
    return jnp.concatenate([square, square], axis=1)


def split3(row):
    high = row.astype(BF16).astype(F32)
    middle = (row - high).astype(BF16).astype(F32)
    return [high, middle, row - high - middle]


def code_of(largest):
    return jnp.ceil(jnp.log2(jnp.maximum(largest, 1e-30)) * 128.0)


def size_of(code):
    return jnp.exp2(code * (1.0 / 128.0))


def to_int16(values):
    return jnp.round(values).astype(jnp.int32).astype(jnp.int16)


def encode_rows(sums):
    rows = []
    for value in sums:
        code = code_of(jnp.abs(value))
        scaled = value / size_of(code) * FULL
        whole = jnp.round(scaled)
        rows += [code, whole, jnp.round((scaled - whole) * 65000.0)]
    return rows


def decode_rows(extra):
    rows = extra[...].astype(jnp.int32).astype(F32)[:, :RHS]
    sums = []
    for at in (4, 7):
        whole = rows[at + 1 : at + 2] + rows[at + 2 : at + 3] * (1.0 / 65000.0)
        sums.append(size_of(rows[at : at + 1]) * whole * (1.0 / FULL))
    return sums


def encode(out, pieces, sums):
    lane = lax.broadcasted_iota(jnp.int32, (RHS, RHS), 1)
    codes = jnp.zeros((RHS, RHS), F32)
    for m, piece in enumerate(pieces):
        code = code_of(jnp.max(jnp.abs(piece), axis=1, keepdims=True))
        out[m * RHS : (m + 1) * RHS] = to_int16(piece * (FULL / size_of(code)))
        codes = jnp.where(lane == m, code, codes)
    rows = jnp.concatenate([codes.T[:4]] + encode_rows(sums) + [jnp.zeros((EXTRA - 10, RHS), F32)], axis=0)
    out[len(pieces) * RHS :] = to_int16(jnp.concatenate([rows, jnp.zeros_like(rows)], axis=1))


def decode(message, count):
    rows = message[count * RHS :].astype(jnp.int32).astype(F32)[:, :RHS]
    square = jnp.concatenate([rows, jnp.zeros((RHS - EXTRA, RHS), F32)], axis=0).T
    pieces = []
    for m in range(count):
        scale = size_of(square[:, m : m + 1]) * (1.0 / FULL)
        pieces.append(message[m * RHS : (m + 1) * RHS].astype(jnp.int32).astype(F32) * scale)
    return pieces


def two_rows(rows):
    return jnp.concatenate([rows[0], rows[1], jnp.zeros((6, RHS), F32)], axis=0)


def live_pair(live, leaf_a, leaf_b):
    return jnp.concatenate([live[pl.ds(leaf_a, 1), :], live[pl.ds(leaf_b, 1), :]], axis=1)


def first_message(data, extra, out):
    out[:RHS] = data[...].T.astype(BF16)
    out[RHS:] = extra[...]


M_ROW, M_HALO, M_OWNER, M_AT, M_ODD, M_COL = 16, 24, 26, 27, 28, 29


def slot_of(meta, column):
    apart = column ^ meta[M_AT]
    swapped = (apart % 4) * 4 + apart // 4
    return jnp.where(meta[M_ODD] == 1, swapped, apart)


def tile_at(tiles, s, k):
    return tiles[s % 4][BAND * (s // 4) + k]


def data_pieces(group, other):
    return [a[:RHS] for a in group] + [other[MSG * m : MSG * m + RHS] for m in range(4)]


def data_extras(group, other):
    return [a[RHS:] for a in group] + [other[MSG * m + RHS : MSG * (m + 1)] for m in range(4)]


def add_near_terms(meta, cols, pieces, tiles, near):
    near[...] = jnp.zeros_like(near)

    @pl.when(meta[M_OWNER] == 1)
    def _():
        for s in range(COLS):
            for k in range(BAND):
                slot = slot_of(meta, cols[s, k])
                near[slot] += nn(pieces[s], tile_at(tiles, s, k))


def far_pair(meta, live, left, right, pieces, slot):
    ja, jb = meta[slot], meta[slot + 1]
    coef_a, coef_b, right_a, right_b = [], [], [], []
    for s in range(COLS):
        base = meta[M_ROW + s] * ROWS
        pair = jnp.concatenate([left[base + ja], left[base + jb]], axis=0)
        coef = (nt(pieces[s], pair) * live_pair(live, base + ja, base + jb)).astype(BF16)
        coef_a.append(coef[:, :RANK])
        coef_b.append(coef[:, RANK:])
        right_a.append(right[base + ja])
        right_b.append(right[base + jb])
    part_a = nn(jnp.concatenate(coef_a, axis=1), jnp.concatenate(right_a, axis=0))
    part_b = nn(jnp.concatenate(coef_b, axis=1), jnp.concatenate(right_b, axis=0))
    return part_a, part_b


def far_group(meta, live, left, right, pieces, m2):
    first = far_pair(meta, live, left, right, pieces, 4 * m2)
    return first + far_pair(meta, live, left, right, pieces, 4 * m2 + 2)


def far_only_kernel(meta, live, left, right, a0, a1, a2, a3, b, far, cols):
    pieces = data_pieces((a0, a1, a2, a3), b)
    rows = [extra.astype(F32)[:1, :RHS] for extra in data_extras((a0, a1, a2, a3), b)]
    cols[...] = jnp.concatenate(rows, axis=0).astype(jnp.int32)
    for m2 in range(4):
        for m1, part in enumerate(far_group(meta, live, left, right, pieces, m2)):
            far[4 * m2 + m1] = part


def near_encode_kernel(meta, cols, far, a0, a1, a2, a3, b, t0, t1, t2, t3, g1, g3, g2, own_out, near):
    add_near_terms(meta, cols, data_pieces((a0, a1, a2, a3), b), (t0, t1, t2, t3), near)
    zero = jnp.zeros((1, RHS), F32)
    for m2, out in ((1, g1), (3, g3), (2, g2)):
        encode(out, [far[4 * m2 + m] + near[4 * m2 + m] for m in range(4)], [zero, zero])
    for m in range(4):
        own_out[m * RHS : (m + 1) * RHS] = far[m] + near[m]


def adjoint_first_kernel(
    meta, cols, reg, live, left, right, a0, a1, a2, a3, b, t0, t1, t2, t3, g1, g3, g2, near, sums_out, rims_out, first, last
):
    pieces = data_pieces((a0, a1, a2, a3), b)
    sums = [jnp.zeros((1, RHS), F32)] * 2
    for s, extra in enumerate(data_extras((a0, a1, a2, a3), b)):
        terms = extra.astype(F32)[:, :RHS]
        sums = [sums[0] + (terms[0:1] + terms[1:2] + terms[2:3]), sums[1] + (terms[3:4] + terms[4:5] + terms[5:6])]
        column = meta[M_ROW + s]
        first[pl.ds(column, 1), :] = terms[6:7]
        last[pl.ds(column, 1), :] = terms[7:8]
    at, column = meta[M_AT], meta[M_COL]
    cross = jnp.sum(last[0 : COLS - 1] * first[1:COLS], axis=0, keepdims=True)
    sums[1] += jnp.where(at == 0, -2.0 * reg[...] * cross, 0.0)
    before = last[pl.ds(jnp.maximum(column - 1, 0), 1), :]
    after = first[pl.ds(jnp.minimum(column + 1, COLS - 1), 1), :]
    rims_out[...] = two_rows(
        [
            jnp.where(column > 0, before, 0.0),
            jnp.where(column < COLS - 1, after, 0.0),
        ]
    )
    sums_out[...] = two_rows(sums)
    add_near_terms(meta, cols, pieces, (t0, t1, t2, t3), near)
    for m2, out in ((1, g1), (3, g3), (2, g2)):
        parts = far_group(meta, live, left, right, pieces, m2)
        encode(out, [part + near[4 * m2 + m] for m, part in enumerate(parts)], sums)


def adjoint_second_kernel(meta, live, left, right, a0, a1, a2, a3, b, near, own_out):
    pieces = data_pieces((a0, a1, a2, a3), b)
    for m, part in enumerate(far_group(meta, live, left, right, pieces, 0)):
        own_out[m * RHS : (m + 1) * RHS] = part + near[m]


def coefficient_pair(meta, live, right, held, s, slots):
    base_a, base_b = meta[M_ROW + s] * ROWS, meta[M_ROW + s + 1] * ROWS
    coef_a, coef_b = [], []
    for slot in slots:
        j = meta[slot]
        pair = jnp.concatenate([right[base_a + j], right[base_b + j]], axis=0)
        coef = (nt(held(slot), pair) * live_pair(live, base_a + j, base_b + j)).astype(BF16)
        coef_a.append(coef[:, :RANK])
        coef_b.append(coef[:, RANK:])
    return jnp.concatenate(coef_a, axis=1), jnp.concatenate(coef_b, axis=1)


def piece_of(arrays):
    def held(slot):
        return arrays[slot // 4][(slot % 4) * RHS : (slot % 4 + 1) * RHS]

    return held


def left_rows(meta, left, s, slots):
    base = meta[M_ROW + s] * ROWS
    return jnp.concatenate([left[base + meta[slot]] for slot in slots], axis=0)


def forward_near_kernel(meta, live, left, right, a, partial):
    for s in (4, 6, 0, 2):
        for at, coef in enumerate(coefficient_pair(meta, live, right, piece_of((a,)), s, range(4))):
            partial[s + at] = nn(coef, left_rows(meta, left, s + at, range(4)))


def forward_rows(meta, cols, live, left, right, partial, arrays, tiles, out, near, held, start):
    piece = piece_of(arrays)
    for slot in range(ROWS):
        held[slot] = piece(slot)
    for m in range(4):
        near[m] = partial[start + m]

    @pl.when(meta[M_OWNER] == 1)
    def _():
        for m in range(4):
            for k in range(BAND):
                slot = slot_of(meta, cols[start + m, k])
                near[m] += nt(held[slot], tile_at(tiles, start + m, k))

    for m in (0, 2):
        s = start + m
        for at, coef in enumerate(coefficient_pair(meta, live, right, piece, s, range(4, ROWS))):
            value = nn(coef, left_rows(meta, left, s + at, range(4, ROWS))) + near[m + at]
            out[(m + at) * RHS : (m + at + 1) * RHS] = value.astype(out.dtype)


def forward_first_kernel(
    meta, cols, live, left, right, partial, a, b1, b2, b3, t0, t1, t2, t3, out, held, near
):
    forward_rows(
        meta, cols, live, left, right, partial, (a, b1, b2, b3), (t0, t1, t2, t3), out, near, held, 4
    )


def forward_second_kernel(
    meta, cols, live, left, right, partial, a, b1, b2, b3, t0, t1, t2, t3, own, out, curved, edges, held, near
):
    forward_rows(
        meta, cols, live, left, right, partial, (a, b1, b2, b3), (t0, t1, t2, t3), out, near, held, 0
    )
    lane = lax.broadcasted_iota(jnp.int32, (RHS, LEAF), 1)
    for m in range(4):
        rows = slice(m * RHS, (m + 1) * RHS)
        vector, j = own[rows], meta[m]
        before = held[slot_of(meta, (j + ROWS - 1) % ROWS)][:, LEAF - RHS :].astype(F32)[:, RHS - 1 :]
        after = held[slot_of(meta, (j + 1) % ROWS)][:, :RHS].astype(F32)[:, :1]
        before = jnp.where(j == 0, 0.0, before)
        after = jnp.where(j == ROWS - 1, 0.0, after)
        below = jnp.where(lane == 0, before, pltpu.roll(vector, 1, 1))
        above = jnp.where(lane == LEAF - 1, after, pltpu.roll(vector, LEAF - 1, 1))
        curved[rows] = 2.0 * vector - below - above
    first = held[slot_of(meta, 0)][:, :RHS].astype(F32).T[:1]
    last = held[slot_of(meta, ROWS - 1)][:, LEAF - RHS :].astype(F32).T[RHS - 1 :]
    edges[...] = two_rows([first, last])


def without_rims(curved, before, after, j):
    lane = lax.broadcasted_iota(jnp.int32, (RHS, LEAF), 1)
    curved = curved - jnp.where((lane == 0) & (j == 0), before, 0.0)
    return curved - jnp.where((lane == LEAF - 1) & (j == ROWS - 1), after, 0.0)


def row_phase_first_kernel(own, g1, g3, g2, own_out, message):
    totals = [own[m * RHS : (m + 1) * RHS] for m in range(4)]
    for g in (g1, g3, g2):
        totals = [x + y for x, y in zip(totals, decode(g, 4))]
    zero = jnp.zeros((1, RHS), F32)
    encode(message, totals, [zero, zero])
    for m in range(4):
        own_out[m * RHS : (m + 1) * RHS] = totals[m]


def row_phase_kernel(own, sums_in, g1, g3, g2, own_out, sums_out, message):
    sums = [sums_in[0:1], sums_in[1:2]]
    totals = [own[m * RHS : (m + 1) * RHS] for m in range(4)]
    for g in (g1, g3, g2):
        sums = [x + y for x, y in zip(sums, decode_rows(g[4 * RHS :]))]
        totals = [x + y for x, y in zip(totals, decode(g, 4))]
    sums_out[...] = two_rows(sums)
    encode(message, totals, sums)
    for m in range(4):
        own_out[m * RHS : (m + 1) * RHS] = totals[m]


def group_totals(own, p1, p3, p2):
    totals = [own[m * RHS : (m + 1) * RHS] for m in range(4)]
    for k, p in ((1, p1), (3, p3), (2, p2)):
        got = decode(p, 4)
        totals = [total + got[k ^ m] for m, total in enumerate(totals)]
    return totals


def descent_kernel(own, p1, p3, p2, full, sent):
    for m, total in enumerate(group_totals(own, p1, p3, p2)):
        full[m * RHS : (m + 1) * RHS] = total
        sent[m * RHS : (m + 1) * RHS] = total.astype(BF16)


def descent2_kernel(meta, reg, first, curved, rims, own, sums_in, p1, p3, p2, full, sent, curved_out, sums_out):
    sums = [sums_in[0:1], sums_in[1:2]]
    for p in (p1, p3, p2):
        sums = [x + y for x, y in zip(sums, decode_rows(p[4 * RHS :]))]
    sums_out[...] = two_rows(sums)
    step, weight = as_column(sums[0] / sums[1]), as_column(reg[...])
    before, after = as_column(rims[0:1]), as_column(rims[1:2])
    for m, total in enumerate(group_totals(own, p1, p3, p2)):
        rows = slice(m * RHS, (m + 1) * RHS)
        whole = without_rims(curved[rows], before, after, meta[m])
        curved_out[rows] = whole
        vector = first[rows] - step * (total + weight * whole)
        full[rows] = vector
        sent[rows] = vector.astype(BF16)


def core_phase_kernel(own, other, own_out, p1, p3, p2):
    for m, out in ((1, p1), (3, p3), (2, p2), (0, own_out)):
        rows = slice(m * RHS, (m + 1) * RHS)
        out[...] = (own[rows] + other[rows].astype(F32)).astype(out.dtype)


def image_kernel(reg, vector, curved, edges, own, p1, p3, p2, full, message):
    total = own[...]
    for p in (p1, p3, p2):
        total += p[...].astype(F32)
    full[...] = total
    value = vector[:RHS]
    message[:RHS] = total.astype(BF16)
    gamma = row_sum(value * value)
    delta = row_sum(total * total) + reg[...] * row_sum(value * curved[:RHS])
    rows = jnp.concatenate(
        split3(gamma) + split3(delta) + [edges[0:2], jnp.zeros((EXTRA - 8, RHS), F32)], axis=0
    )
    message[RHS:] = jnp.concatenate([rows, jnp.zeros_like(rows)], axis=1).astype(BF16)


def image2_kernel(meta, reg, vector, curved, edges, curved_first, first, own, p1, p3, p2, full, sums):
    total = own[...]
    for p in (p1, p3, p2):
        total += p[...].astype(F32)
    full[...] = total
    value = vector[:RHS]
    weight = reg[...]
    sums[...] = jnp.zeros_like(sums)
    sums[0:1] = row_sum(value * value)
    sums[1:2] = row_sum(total * total) + weight * row_sum(value * curved[:RHS])
    sums[2:3] = row_sum(total * first[...]) + weight * row_sum(value * curved_first[:RHS])
    column = meta[M_COL]
    sums[pl.ds(8 + column, 1), :] = jnp.where(meta[M_AT] == 0, edges[0:1], 0.0)
    sums[pl.ds(16 + column, 1), :] = jnp.where(meta[M_AT] == 0, edges[1:2], 0.0)


def repeat_kernel(own, p1, p3, p2, out):
    total = own[...] + p1[...] + (p3[...] + p2[...])
    for k in range(ROWS):
        out[k * SUMS : (k + 1) * SUMS] = total


def transposed_kernel(*refs):
    sources, near, outs, (held, sems) = refs[:4], refs[4:6], refs[6:12], refs[12:]
    copies = [
        pltpu.make_async_copy(source.at[pl.ds(0, RHS)], held.at[k], sems.at[k]) for k, source in enumerate(sources)
    ]
    for copy in copies:
        copy.start()
    for value, out in zip(near, outs[4:]):
        out[...] = value[...].T
    for k, copy in enumerate(copies):
        copy.wait()
        outs[k][...] = held[k].T


def final_kernel(meta, reg, sums1, gathered, s1, s2, d1, d2, y1, y2, data, solution_out, misfit_out, curved_out, held):
    total = gathered[:SUMS]
    for k in range(1, ROWS):
        total += gathered[k * SUMS : (k + 1) * SUMS]
    held[...] = total
    gamma, delta = sums1[0:1], sums1[1:2]
    first, last = held[8 : 8 + COLS], held[16 : 16 + COLS]
    cross = jnp.sum(last[: COLS - 1] * first[1:], axis=0, keepdims=True)
    fresh, delta_new, delta_mixed = held[0:1], held[1:2] - 2.0 * reg[...] * cross, held[2:3]
    at, column = meta[M_AT], meta[M_COL]
    before = held[pl.ds(16 + jnp.maximum(column - 1, 0), 1), :]
    after = held[pl.ds(8 + jnp.minimum(column + 1, COLS - 1), 1), :]
    row = lax.broadcasted_iota(jnp.int32, (LEAF, RHS), 0)
    curved = d2[...] - jnp.where((row == 0) & (at == 0) & (column > 0), before, 0.0)
    curved -= jnp.where((row == LEAF - 1) & (at == ROWS - 1) & (column < COLS - 1), after, 0.0)
    beta = fresh / gamma
    delta2 = delta_new + 2.0 * beta * delta_mixed + beta * beta * delta
    two = fresh / delta2
    one = gamma / delta + two * beta
    solution_out[...] = one * s1[...] + two * s2[...]
    curved_out[...] = one * d1[...] + two * curved
    misfit_out[...] = data[...] - (one * y1[...] + two * y2[...])


def grid_pairs(move):
    return [(r * COLS + c, to) for r in range(ROWS) for c in range(COLS) for to in [move(r, c)] if to is not None]


def send(value, move):
    return lax.ppermute(value, ("row", "col"), grid_pairs(move))


def near_move(m):
    return lambda r, c: (r ^ (m if c % 2 == 0 else 4 * m)) * COLS + c


def far_move(m):
    return lambda r, c: (r ^ (4 * m if c % 2 == 0 else m)) * COLS + c


def y_move(m):
    return lambda r, c: r * COLS + (c ^ (2 * m))


def core_move(r, c):
    return r * COLS + (c ^ 1)


def tile_core_move(r, c):
    return r * COLS + (c ^ 1) if c % 2 != (r // 2) % 2 else None


def tile_move(m):
    def move(r, c):
        owner = r // 2
        there = c % 2 == owner % 2 and (c // 2) ^ (owner // 2) == m
        return r * COLS + (c ^ (2 * m)) if there else None

    return move


def per_device(far_left, far_right, far_rank, near_tiles, near_cols, data, reg_weight):
    r = lax.axis_index("row")
    c = lax.axis_index("col")
    odd = c % 2
    leaves = far_rank.shape[-1]

    def at_slot(m2, m1):
        return jnp.where(odd == 0, r ^ m1 ^ (4 * m2), r ^ (4 * m1) ^ m2)

    def slot_at(column):
        apart = column ^ r
        return jnp.where(odd == 1, (apart % 4) * 4 + apart // 4, apart)

    meta = jnp.stack(
        [at_slot(s // 4, s % 4) for s in range(ROWS)]
        + [c ^ (2 * (s % 4)) ^ (s // 4) for s in range(COLS)]
        + [slot_at((r + ROWS - 1) % ROWS), slot_at((r + 1) % ROWS)]
        + [(c == r // 2).astype(jnp.int32), r, odd, c]
    ).astype(jnp.int32)
    reg = reg_weight.reshape(1, RHS)
    data = data.reshape(LEAF, RHS)

    cols_row = jnp.pad(near_cols.astype(BF16), ((0, EXTRA - 1), (0, LEAF - BAND)))
    message = call(first_message, shape((MSG, LEAF), BF16), data, cols_row)

    def gather_col_pieces(mine):
        got = {m: send(mine, y_move(m)) for m in ORDER}
        return [mine, got[1], got[2], got[3]]

    group = gather_col_pieces(message)
    tiles = near_tiles.reshape(BAND, LEAF, LEAF)
    tiles = jnp.concatenate([tiles, send(tiles, tile_core_move)], axis=0)
    tiles = [tiles] + [send(tiles, tile_move(m)) for m in (1, 2, 3)]
    left = far_left.reshape(leaves, RANK, LEAF)
    right = far_right.reshape(leaves, RANK, LEAF)
    live = (lax.broadcasted_iota(jnp.int32, (leaves, RANK), 1) < far_rank.reshape(leaves, 1)).astype(F32)
    other = send(jnp.concatenate(group, axis=0), core_move)

    def factors():
        return [live] + [pltpu.with_memory_space_constraint(x, pltpu.VMEM) for x in (left, right)]

    vec, sums_shape = shape((RHS, LEAF)), shape((8, RHS))
    sent_shape = shape((RHS, LEAF), BF16)
    group4, group4_sent = shape((4 * RHS, LEAF)), shape((4 * RHS, LEAF), BF16)
    big = shape((4 * RHS + EXTRA, LEAF), jnp.int16)
    near_shape = shape((ROWS, RHS, LEAF))
    near_scratch = pltpu.VMEM((ROWS, RHS, LEAF), F32)

    def specs(scalars, vectors):
        return [SMEM] * scalars + [VMEM] * vectors

    def sum_over_row(own, sums, parts):
        got = [send(g, far_move(m)) for m, g in zip(ORDER, parts)]
        if sums is None:
            own, message = call(row_phase_first_kernel, (group4, big), own, *got)
        else:
            own, sums, message = call(row_phase_kernel, (group4, sums_shape, big), own, sums, *got)
        return own, sums, [send(message, near_move(m)) for m in ORDER]

    def product(vector, sent):
        got = {m: send(sent, far_move(m)) for m in ORDER}
        pieces = [sent, got[1], got[2], got[3]]
        partial = call(
            forward_near_kernel, shape((COLS, RHS, LEAF)), meta, *factors(), sent, specs=specs(1, 4), flops=1 << 29
        )
        scratch = [pltpu.VMEM((ROWS, RHS, LEAF), BF16), pltpu.VMEM((4, RHS, LEAF), F32)]
        parts = call(
            forward_first_kernel, group4_sent, meta, cols, *factors(), partial, *pieces, *tiles,
            specs=specs(2, 12), scratch=scratch, flops=1 << 30,
        )
        other = send(parts, core_move)
        own, curved, edges = call(
            forward_second_kernel, (group4, group4, sums_shape), meta, cols, *factors(), partial, *pieces, *tiles, vector,
            specs=specs(2, 13), scratch=scratch, flops=1 << 30,
        )
        own, p1, p3, p2 = call(core_phase_kernel, (vec, sent_shape, sent_shape, sent_shape), own, other)
        return curved, edges, [own] + [send(p, y_move(m)) for m, p in zip(ORDER, (p1, p3, p2))]

    far, cols = call(
        far_only_kernel, (near_shape, shape((COLS, RHS), jnp.int32)), meta, *factors(), *group, other,
        specs=specs(1, 8), flops=1 << 32,
    )
    g1, g3, g2, own = call(
        near_encode_kernel, (big, big, big, group4), meta, cols, far, *group, other, *tiles,
        specs=specs(2, 10), scratch=[near_scratch], flops=1 << 29,
    )
    own, _, parts = sum_over_row(own, None, (g1, g3, g2))
    s1, s1_sent = call(descent_kernel, (group4, group4_sent), own, *parts)
    d1, edges, parts = product(s1, s1_sent)
    y1, message = call(image_kernel, (vec, shape((MSG, LEAF), BF16)), reg, s1, d1, edges, *parts)

    group = gather_col_pieces(message)
    other = send(jnp.concatenate(group, axis=0), core_move)
    g1, g3, g2, near, sums, rims = call(
        adjoint_first_kernel, (big, big, big, near_shape, sums_shape, sums_shape),
        meta, cols, reg, *factors(), *group, other, *tiles,
        specs=specs(2, 13), scratch=[pltpu.VMEM((COLS, RHS), F32)] * 2, flops=1 << 30,
    )
    own = call(
        adjoint_second_kernel, group4, meta, *factors(), *group, other, near,
        specs=specs(1, 9), flops=1 << 30,
    )
    own, sums, parts = sum_over_row(own, sums, (g1, g3, g2))
    s2, s2_sent, d1, sums1 = call(
        descent2_kernel, (group4, group4_sent, group4, sums_shape), meta, reg, s1, d1, rims, own, sums, *parts,
        specs=specs(1, 9),
    )
    d2, edges, parts = product(s2, s2_sent)
    y2, sums2 = call(
        image2_kernel, (vec, shape((SUMS, RHS))), meta, reg, s2, d2, edges, d1, y1, *parts, specs=specs(1, 10)
    )
    sums2 = sums2 + send(sums2, core_move)
    got = [send(sums2, y_move(m)) for m in ORDER]
    repeated = call(repeat_kernel, shape((ROWS * SUMS, RHS)), sums2, *got)
    gathered = lax.all_to_all(repeated, "row", 0, 0, tiled=True)
    piece = shape((LEAF, RHS))
    in_hbm = [pltpu.with_memory_space_constraint(x, pltpu.HBM) for x in (s1, s2, d1, d2)]
    ready = call(
        transposed_kernel, (piece,) * 6, *in_hbm, y1, y2, specs=[HBM] * 4 + [VMEM] * 2,
        scratch=[pltpu.VMEM((4, RHS, LEAF), F32), pltpu.SemaphoreType.DMA((4,))],
    )
    solution_out, misfit_out, curved_out = call(
        final_kernel, (piece, piece, piece), meta, reg, sums1, gathered, *ready, data,
        specs=specs(1, 10), scratch=[pltpu.VMEM((SUMS, RHS), F32)],
    )
    whole = (1, 1, LEAF, RHS)
    return solution_out.reshape(whole), misfit_out.reshape(whole), curved_out.reshape(whole)


def solution(mesh):
    in_specs = (
        P("row", "col", None, None, None),
        P("row", "col", None, None, None),
        P("row", "col", None),
        P(("row", "col"), None, None, None),
        P(("row", "col"), None),
        P("row", "col", None, None),
        P(),
    )
    out_specs = (
        P("col", "row", None, None),
        P("row", "col", None, None),
        P("col", "row", None, None),
    )
    return jax.shard_map(
        per_device, mesh=mesh, in_specs=in_specs, out_specs=out_specs, check_vma=False
    )
```

profile of v0, /device:TPU:0, one launch (start us, length us, event | category | flops | bytes accessed | tf_op | source)
XLA Modules:
  0.0 171.8 jit_solution(8069512283295719949)
XLA Ops:
  3.6 3.2 %collective-permute-start.2 = (bf16[144,256]{1,0:T(8,128)(2,1)S(1)}, bf16[144,256]{1,0:T(8,128)(2,1)S(1)}, u32[]{:S(2)}, u32[]{:S(2)}) collective-permute-start(bf16[144,256]{1,0:T(8,128)(2,1)S(1)} %shard_map.94.a0), channel_id=1, source_target_pairs={{0,6},{1,7},{2,4},{3,5},{4,2},{5,3},{6,0},{7,1},{8,14},{9,15},{10,... | collective-permute-start | bytes 221192 | tf_op jit(solution)/shard_map/ppermute | solution.py:462
  16.6 3.4 %copy-done = bf16[1,1,128,128,256]{4,3,2,1,0:T(8,128)(2,1)S(1)} copy-done((bf16[1,1,128,128,256]{4,3,2,1,0:T(8,128)(2,1)S(1)}, bf16[1,1,128,128,256]{4,3,2,1,0:T(8,128)(2,1)}, u32[]{:S(2)}) %copy-start) | copy-done | bytes 8388632
  20.0 3.4 %copy-done.2 = bf16[1,1,128,128,256]{4,3,2,1,0:T(8,128)(2,1)S(1)} copy-done((bf16[1,1,128,128,256]{4,3,2,1,0:T(8,128)(2,1)S(1)}, bf16[1,1,128,128,256]{4,3,2,1,0:T(8,128)(2,1)}, u32[]{:S(2)}) %copy-start.2) | copy-done | bytes 8388632
  26.1 4.7 %shard_map.95 = (f32[16,128,256]{2,1,0:T(8,128)S(1)}, s32[8,128]{1,0:T(8,128)S(1)}) custom-call(s32[30]{0:T(128)S(1)} %stack.121.meta, f32[128,128]{1,0:T(8,128)S(1)} %fusion.live, bf16[128,128,256]{2,1,0:T(8,128)(2,1)S(1)} %bitcast.39, bf16[128,128,256]{2,1,0:T(8,128)(2,1)S(1)} %bitcast.48, bf16[144,256]{1,0:T(8,128)(2,1)S(1)} %shard_map.94.a0, ...), custom_call_target="tpu_custom_call" | custom-call | flops 4294967296 | bytes 65536 | tf_op jit(solution)/shard_map/pallas_call | solution.py:31
  35.4 3.1 %collective-permute-start.9 = (s16[528,256]{1,0:T(8,128)(2,1)S(1)}, s16[528,256]{1,0:T(8,128)(2,1)S(1)}, u32[]{:S(2)}, u32[]{:S(2)}) collective-permute-start(s16[528,256]{1,0:T(8,128)(2,1)S(1)} %get-tuple-element.57), channel_id=1, source_target_pairs={{0,96},{1,25},{2,98},{3,27},{4,100},{5,29},{6,102},{7,31},{8,104},... | collective-permute-start | bytes 811016 | tf_op jit(solution)/shard_map/ppermute | solution.py:462
  40.9 4.5 %collective-permute-done.9.g3 = s16[528,256]{1,0:T(8,128)(2,1)S(1)} collective-permute-done((s16[528,256]{1,0:T(8,128)(2,1)S(1)}, s16[528,256]{1,0:T(8,128)(2,1)S(1)}, u32[]{:S(2)}, u32[]{:S(2)}) %collective-permute-start.9) | collective-permute-done | bytes 270368 | tf_op jit(solution)/shard_map/ppermute | solution.py:462
  51.8 3.5 %collective-permute-done.13.p2 = s16[528,256]{1,0:T(8,128)(2,1)S(1)} collective-permute-done((s16[528,256]{1,0:T(8,128)(2,1)S(1)}, s16[528,256]{1,0:T(8,128)(2,1)S(1)}, u32[]{:S(2)}, u32[]{:S(2)}) %collective-permute-start.13) | collective-permute-done | bytes 270368 | tf_op jit(solution)/shard_map/ppermute | solution.py:462
  55.3 2.8 %collective-permute-done.12.p3 = s16[528,256]{1,0:T(8,128)(2,1)S(1)} collective-permute-done((s16[528,256]{1,0:T(8,128)(2,1)S(1)}, s16[528,256]{1,0:T(8,128)(2,1)S(1)}, u32[]{:S(2)}, u32[]{:S(2)}) %collective-permute-start.12) | collective-permute-done | bytes 270368 | tf_op jit(solution)/shard_map/ppermute | solution.py:462
  64.8 3.3 %collective-permute-done.16.b3 = bf16[512,256]{1,0:T(8,128)(2,1)S(1)} collective-permute-done((bf16[512,256]{1,0:T(8,128)(2,1)S(1)}, bf16[512,256]{1,0:T(8,128)(2,1)S(1)}, u32[]{:S(2)}, u32[]{:S(2)}) %collective-permute-start.16) | collective-permute-done | bytes 262176 | tf_op jit(solution)/shard_map/ppermute | solution.py:462
  70.1 3.2 %shard_map.101 = bf16[512,256]{1,0:T(8,128)(2,1)S(1)} custom-call(s32[30]{0:T(128)S(1)} %stack.121.meta, s32[8,128]{1,0:T(8,128)S(1)} %get-tuple-element.53.cols, f32[128,128]{1,0:T(8,128)S(1)} %fusion.live, bf16[128,128,256]{2,1,0:T(8,128)(2,1)S(1)} %bitcast.41, bf16[128,128,256]{2,1,0:T(8,128)(2,1)S(1)} %bitcast.50, f32[8,128,256]{2,1,0:T(8,128)S(1)} %shard_map.99.partial, ...), custom_call_target="tpu_custom_call" | custom-call | flops 1073741824 | bytes 65536 | tf_op jit(solution)/shard_map/pallas_call | solution.py:31
  73.4 3.1 %shard_map.100 = (f32[512,256]{1,0:T(8,128)S(1)}, f32[512,256]{1,0:T(8,128)S(1)}, f32[8,128]{1,0:T(8,128)S(1)}) custom-call(s32[30]{0:T(128)S(1)} %stack.121.meta, s32[8,128]{1,0:T(8,128)S(1)} %get-tuple-element.53.cols, f32[128,128]{1,0:T(8,128)S(1)} %fusion.live, bf16[128,128,256]{2,1,0:T(8,128)(2,1)S(1)} %bitcast.42, bf16[128,128,256]{2,1,0:T(8,128)(2,1)S(1)} %bitcast.51, ...), custom_call_target="tpu_custom_call" | custom-call | flops 1073741824 | bytes 65536 | tf_op jit(solution)/shard_map/pallas_call | solution.py:31
  78.1 2.7 %collective-permute-start.20 = (bf16[128,256]{1,0:T(8,128)(2,1)S(1)}, bf16[128,256]{1,0:T(8,128)(2,1)S(1)}, u32[]{:S(2)}, u32[]{:S(2)}) collective-permute-start(bf16[128,256]{1,0:T(8,128)(2,1)S(1)} %get-tuple-element.69), channel_id=1, source_target_pairs={{0,4},{1,5},{2,6},{3,7},{4,0},{5,1},{6,2},{7,3},{8,12},{9,13},{10,... | collective-permute-start | bytes 196616 | tf_op jit(solution)/shard_map/ppermute | solution.py:462
  93.6 4.9 %shard_map.104 = (s16[528,256]{1,0:T(8,128)(2,1)S(1)}, s16[528,256]{1,0:T(8,128)(2,1)S(1)}, s16[528,256]{1,0:T(8,128)(2,1)S(1)}, f32[16,128,256]{2,1,0:T(8,128)S...) custom-call(s32[30]{0:T(128)S(1)} %stack.121.meta, s32[8,128]{1,0:T(8,128)S(1)} %get-tuple-element.53.cols, ...), custom_call_target="tpu_custom_call" | custom-call | flops 1073741824 | bytes 65536 | tf_op jit(solution)/shard_map/pallas_call | solution.py:31
  105.0 3.0 %collective-permute-done.26.g3 = s16[528,256]{1,0:T(8,128)(2,1)S(1)} collective-permute-done((s16[528,256]{1,0:T(8,128)(2,1)S(1)}, s16[528,256]{1,0:T(8,128)(2,1)S(1)}, u32[]{:S(2)}, u32[]{:S(2)}) %collective-permute-start.26) | collective-permute-done | bytes 270368 | tf_op jit(solution)/shard_map/ppermute | solution.py:462
  112.2 2.9 %collective-permute-start.29 = (s16[528,256]{1,0:T(8,128)(2,1)S(1)}, s16[528,256]{1,0:T(8,128)(2,1)S(1)}, u32[]{:S(2)}, u32[]{:S(2)}) collective-permute-start(s16[528,256]{1,0:T(8,128)(2,1)S(1)} %get-tuple-element.79), channel_id=1, source_target_pairs={{0,24},{1,97},{2,26},{3,99},{4,28},{5,101},{6,30},{7,103},{8,16},{... | collective-permute-start | bytes 811016 | tf_op jit(solution)/shard_map/ppermute | solution.py:462
  115.1 3.6 %collective-permute-done.30.p2 = s16[528,256]{1,0:T(8,128)(2,1)S(1)} collective-permute-done((s16[528,256]{1,0:T(8,128)(2,1)S(1)}, s16[528,256]{1,0:T(8,128)(2,1)S(1)}, u32[]{:S(2)}, u32[]{:S(2)}) %collective-permute-start.30) | collective-permute-done | bytes 270368 | tf_op jit(solution)/shard_map/ppermute | solution.py:462
  118.6 2.8 %collective-permute-done.29.p3 = s16[528,256]{1,0:T(8,128)(2,1)S(1)} collective-permute-done((s16[528,256]{1,0:T(8,128)(2,1)S(1)}, s16[528,256]{1,0:T(8,128)(2,1)S(1)}, u32[]{:S(2)}, u32[]{:S(2)}) %collective-permute-start.29) | collective-permute-done | bytes 270368 | tf_op jit(solution)/shard_map/ppermute | solution.py:462
  128.8 4.4 %collective-permute-done.33.b3 = bf16[512,256]{1,0:T(8,128)(2,1)S(1)} collective-permute-done((bf16[512,256]{1,0:T(8,128)(2,1)S(1)}, bf16[512,256]{1,0:T(8,128)(2,1)S(1)}, u32[]{:S(2)}, u32[]{:S(2)}) %collective-permute-start.33) | collective-permute-done | bytes 262176 | tf_op jit(solution)/shard_map/ppermute | solution.py:462
  134.2 3.0 %shard_map.110 = bf16[512,256]{1,0:T(8,128)(2,1)S(1)} custom-call(s32[30]{0:T(128)S(1)} %stack.121.meta, s32[8,128]{1,0:T(8,128)S(1)} %get-tuple-element.53.cols, f32[128,128]{1,0:T(8,128)S(1)} %fusion.live, bf16[128,128,256]{2,1,0:T(8,128)(2,1)S(1)} %bitcast.46, bf16[128,128,256]{2,1,0:T(8,128)(2,1)S(1)} %bitcast.55, ...), custom_call_target="tpu_custom_call" | custom-call | flops 1073741824 | bytes 65536 | tf_op jit(solution)/shard_map/pallas_call | solution.py:31
  137.3 3.1 %shard_map.109 = (f32[512,256]{1,0:T(8,128)S(1)}, f32[512,256]{1,0:T(8,128)S(1)}, f32[8,128]{1,0:T(8,128)S(1)}) custom-call(s32[30]{0:T(128)S(1)} %stack.121.meta, s32[8,128]{1,0:T(8,128)S(1)} %get-tuple-element.53.cols, f32[128,128]{1,0:T(8,128)S(1)} %fusion.live, bf16[128,128,256]{2,1,0:T(8,128)(2,1)S(1)} %bitcast.47, bf16[128,128,256]{2,1,0:T(8,128)(2,1)S(1)} %bitcast.56, ...), custom_call_target="tpu_custom_call" | custom-call | flops 1073741824 | bytes 65536 | tf_op jit(solution)/shard_map/pallas_call | solution.py:31
  141.9 2.8 %collective-permute-start.37 = (bf16[128,256]{1,0:T(8,128)(2,1)S(1)}, bf16[128,256]{1,0:T(8,128)(2,1)S(1)}, u32[]{:S(2)}, u32[]{:S(2)}) collective-permute-start(bf16[128,256]{1,0:T(8,128)(2,1)S(1)} %get-tuple-element.91), channel_id=1, source_target_pairs={{0,4},{1,5},{2,6},{3,7},{4,0},{5,1},{6,2},{7,3},{8,12},{9,13},{10,... | collective-permute-start | bytes 196616 | tf_op jit(solution)/shard_map/ppermute | solution.py:462
  149.6 2.8 %collective-permute-start.41 = (f32[24,128]{1,0:T(8,128)S(1)}, f32[24,128]{1,0:T(8,128)S(1)}, u32[]{:S(2)}, u32[]{:S(2)}) collective-permute-start(f32[24,128]{1,0:T(8,128)S(1)} %add.45.own), channel_id=1, source_target_pairs={{0,4},{1,5},{2,6},{3,7},{4,0},{5,1},{6,2},{7,3},{8,12},{9,13},{10,... | collective-permute-start | bytes 36872 | tf_op jit(solution)/shard_map/ppermute | solution.py:462
  158.0 4.4 %all-to-all-start = ((f32[16,24,128]{2,1,0:T(8,128)}), f32[16,24,128]{2,1,0:T(8,128)S(1)}, u32[]{:S(2)}, u32[]{:S(2)}) async-start(f32[16,24,128]{2,1,0:T(8,128)} %bitcast.34), calls=%async_computation | async-start | bytes 393216 | tf_op jit(solution)/shard_map/all_to_all | solution.py:608
  163.7 6.7 %all-to-all-done = f32[16,24,128]{2,1,0:T(8,128)S(1)} async-done(((f32[16,24,128]{2,1,0:T(8,128)}), f32[16,24,128]{2,1,0:T(8,128)S(1)}, u32[]{:S(2)}, u32[]{:S(2)}) %all-to-all-start) | async-done | bytes 196640 | tf_op jit(solution)/shard_map/all_to_all | solution.py:608
  (126 shorter events, 85.6 us)
Async XLA Ops:
  0.6 7.2 %collective-permute-start.4 = (bf16[3,256,256]{2,1,0:T(8,128)(2,1)}, bf16[3,256,256]{2,1,0:T(8,128)(2,1)S(1)}, u32[]{:S(2)}, u32[]{:S(2)}) collective-permute-start(bf16[3,256,256]{2,1,0:T(8,128)(2,1)} %bitcast.65), channel_id=1, source_target_pairs={{1,0},{3,2},{5,4},{7,6},{9,8},{11,10},{13,12},{15,14},{16,17},{18,... | collective-permute-start | bytes 1179656 | tf_op jit(solution)/shard_map/ppermute | solution.py:462
  3.6 7.8 %collective-permute-start.2 = (bf16[144,256]{1,0:T(8,128)(2,1)S(1)}, bf16[144,256]{1,0:T(8,128)(2,1)S(1)}, u32[]{:S(2)}, u32[]{:S(2)}) collective-permute-start(bf16[144,256]{1,0:T(8,128)(2,1)S(1)} %shard_map.94.a0), channel_id=1, source_target_pairs={{0,6},{1,7},{2,4},{3,5},{4,2},{5,3},{6,0},{7,1},{8,14},{9,15},{10,... | collective-permute-start | bytes 221192 | tf_op jit(solution)/shard_map/ppermute | solution.py:462
  6.8 6.6 %collective-permute-start.1 = (bf16[144,256]{1,0:T(8,128)(2,1)S(1)}, bf16[144,256]{1,0:T(8,128)(2,1)S(1)}, u32[]{:S(2)}, u32[]{:S(2)}) collective-permute-start(bf16[144,256]{1,0:T(8,128)(2,1)S(1)} %shard_map.94.a0), channel_id=1, source_target_pairs={{0,4},{1,5},{2,6},{3,7},{4,0},{5,1},{6,2},{7,3},{8,12},{9,13},{10,... | collective-permute-start | bytes 221192 | tf_op jit(solution)/shard_map/ppermute | solution.py:462
  8.9 23.5 %collective-permute-start.7 = (bf16[6,256,256]{2,1,0:T(8,128)(2,1)S(1)}, bf16[6,256,256]{2,1,0:T(8,128)(2,1)S(1)}, u32[]{:S(2)}, u32[]{:S(2)}) collective-permute-start(bf16[6,256,256]{2,1,0:T(8,128)(2,1)S(1)} %pad_maximum_fusion.t0), channel_id=1, source_target_pairs={{6,0},{14,8},{23,17},{31,25},{36,34},{44,42},{53,51},{61,59},{66,6... | collective-permute-start | bytes 2359304 | tf_op jit(solution)/shard_map/ppermute | solution.py:462
  10.2 22.2 %collective-permute-start.6 = (bf16[6,256,256]{2,1,0:T(8,128)(2,1)S(1)}, bf16[6,256,256]{2,1,0:T(8,128)(2,1)S(1)}, u32[]{:S(2)}, u32[]{:S(2)}) collective-permute-start(bf16[6,256,256]{2,1,0:T(8,128)(2,1)S(1)} %pad_maximum_fusion.t0), channel_id=1, source_target_pairs={{4,0},{12,8},{21,17},{29,25},{38,34},{46,42},{55,51},{63,59},{64,6... | collective-permute-start | bytes 2359304 | tf_op jit(solution)/shard_map/ppermute | solution.py:462
  11.5 20.9 %collective-permute-start.5 = (bf16[6,256,256]{2,1,0:T(8,128)(2,1)S(1)}, bf16[6,256,256]{2,1,0:T(8,128)(2,1)S(1)}, u32[]{:S(2)}, u32[]{:S(2)}) collective-permute-start(bf16[6,256,256]{2,1,0:T(8,128)(2,1)S(1)} %pad_maximum_fusion.t0), channel_id=1, source_target_pairs={{2,0},{10,8},{19,17},{27,25},{32,34},{40,42},{49,51},{57,59},{70,6... | collective-permute-start | bytes 2359304 | tf_op jit(solution)/shard_map/ppermute | solution.py:462
  34.4 6.5 %collective-permute-start.8 = (s16[528,256]{1,0:T(8,128)(2,1)S(1)}, s16[528,256]{1,0:T(8,128)(2,1)S(1)}, u32[]{:S(2)}, u32[]{:S(2)}) collective-permute-start(s16[528,256]{1,0:T(8,128)(2,1)S(1)} %get-tuple-element.56), channel_id=1, source_target_pairs={{0,32},{1,9},{2,34},{3,11},{4,36},{5,13},{6,38},{7,15},{8,40},{9,1... | collective-permute-start | bytes 811016 | tf_op jit(solution)/shard_map/ppermute | solution.py:462
  35.4 10.0 %collective-permute-start.9 = (s16[528,256]{1,0:T(8,128)(2,1)S(1)}, s16[528,256]{1,0:T(8,128)(2,1)S(1)}, u32[]{:S(2)}, u32[]{:S(2)}) collective-permute-start(s16[528,256]{1,0:T(8,128)(2,1)S(1)} %get-tuple-element.57), channel_id=1, source_target_pairs={{0,96},{1,25},{2,98},{3,27},{4,100},{5,29},{6,102},{7,31},{8,104},... | collective-permute-start | bytes 811016 | tf_op jit(solution)/shard_map/ppermute | solution.py:462
  38.5 8.0 %collective-permute-start.10 = (s16[528,256]{1,0:T(8,128)(2,1)S(1)}, s16[528,256]{1,0:T(8,128)(2,1)S(1)}, u32[]{:S(2)}, u32[]{:S(2)}) collective-permute-start(s16[528,256]{1,0:T(8,128)(2,1)S(1)} %get-tuple-element.58), channel_id=1, source_target_pairs={{0,64},{1,17},{2,66},{3,19},{4,68},{5,21},{6,70},{7,23},{8,72},{9,... | collective-permute-start | bytes 811016 | tf_op jit(solution)/shard_map/ppermute | solution.py:462
  47.2 8.1 %collective-permute-start.13 = (s16[528,256]{1,0:T(8,128)(2,1)S(1)}, s16[528,256]{1,0:T(8,128)(2,1)S(1)}, u32[]{:S(2)}, u32[]{:S(2)}) collective-permute-start(s16[528,256]{1,0:T(8,128)(2,1)S(1)} %get-tuple-element.60), channel_id=1, source_target_pairs={{0,16},{1,65},{2,18},{3,67},{4,20},{5,69},{6,22},{7,71},{8,24},{9,... | collective-permute-start | bytes 811016 | tf_op jit(solution)/shard_map/ppermute | solution.py:462
  49.4 8.7 %collective-permute-start.12 = (s16[528,256]{1,0:T(8,128)(2,1)S(1)}, s16[528,256]{1,0:T(8,128)(2,1)S(1)}, u32[]{:S(2)}, u32[]{:S(2)}) collective-permute-start(s16[528,256]{1,0:T(8,128)(2,1)S(1)} %get-tuple-element.60), channel_id=1, source_target_pairs={{0,24},{1,97},{2,26},{3,99},{4,28},{5,101},{6,30},{7,103},{8,16},{... | collective-permute-start | bytes 811016 | tf_op jit(solution)/shard_map/ppermute | solution.py:462
  58.7 9.4 %collective-permute-start.16 = (bf16[512,256]{1,0:T(8,128)(2,1)S(1)}, bf16[512,256]{1,0:T(8,128)(2,1)S(1)}, u32[]{:S(2)}, u32[]{:S(2)}) collective-permute-start(bf16[512,256]{1,0:T(8,128)(2,1)S(1)} %get-tuple-element.62.a), channel_id=1, source_target_pairs={{0,96},{1,25},{2,98},{3,27},{4,100},{5,29},{6,102},{7,31},{8,104},... | collective-permute-start | bytes 786440 | tf_op jit(solution)/shard_map/ppermute | solution.py:462
  61.4 7.9 %collective-permute-start.15 = (bf16[512,256]{1,0:T(8,128)(2,1)S(1)}, bf16[512,256]{1,0:T(8,128)(2,1)S(1)}, u32[]{:S(2)}, u32[]{:S(2)}) collective-permute-start(bf16[512,256]{1,0:T(8,128)(2,1)S(1)} %get-tuple-element.62.a), channel_id=1, source_target_pairs={{0,64},{1,17},{2,66},{3,19},{4,68},{5,21},{6,70},{7,23},{8,72},{9,... | collective-permute-start | bytes 786440 | tf_op jit(solution)/shard_map/ppermute | solution.py:462
  61.4 8.7 %collective-permute-start.14 = (bf16[512,256]{1,0:T(8,128)(2,1)S(1)}, bf16[512,256]{1,0:T(8,128)(2,1)S(1)}, u32[]{:S(2)}, u32[]{:S(2)}) collective-permute-start(bf16[512,256]{1,0:T(8,128)(2,1)S(1)} %get-tuple-element.62.a), channel_id=1, source_target_pairs={{0,32},{1,9},{2,34},{3,11},{4,36},{5,13},{6,38},{7,15},{8,40},{9,1... | collective-permute-start | bytes 786440 | tf_op jit(solution)/shard_map/ppermute | solution.py:462
  98.5 6.5 %collective-permute-start.25 = (s16[528,256]{1,0:T(8,128)(2,1)S(1)}, s16[528,256]{1,0:T(8,128)(2,1)S(1)}, u32[]{:S(2)}, u32[]{:S(2)}) collective-permute-start(s16[528,256]{1,0:T(8,128)(2,1)S(1)} %get-tuple-element.74), channel_id=1, source_target_pairs={{0,32},{1,9},{2,34},{3,11},{4,36},{5,13},{6,38},{7,15},{8,40},{9,1... | collective-permute-start | bytes 811016 | tf_op jit(solution)/shard_map/ppermute | solution.py:462
  99.1 8.9 %collective-permute-start.26 = (s16[528,256]{1,0:T(8,128)(2,1)S(1)}, s16[528,256]{1,0:T(8,128)(2,1)S(1)}, u32[]{:S(2)}, u32[]{:S(2)}) collective-permute-start(s16[528,256]{1,0:T(8,128)(2,1)S(1)} %get-tuple-element.75), channel_id=1, source_target_pairs={{0,96},{1,25},{2,98},{3,27},{4,100},{5,29},{6,102},{7,31},{8,104},... | collective-permute-start | bytes 811016 | tf_op jit(solution)/shard_map/ppermute | solution.py:462
  101.1 8.7 %collective-permute-start.27 = (s16[528,256]{1,0:T(8,128)(2,1)S(1)}, s16[528,256]{1,0:T(8,128)(2,1)S(1)}, u32[]{:S(2)}, u32[]{:S(2)}) collective-permute-start(s16[528,256]{1,0:T(8,128)(2,1)S(1)} %get-tuple-element.76), channel_id=1, source_target_pairs={{0,64},{1,17},{2,66},{3,19},{4,68},{5,21},{6,70},{7,23},{8,72},{9,... | collective-permute-start | bytes 811016 | tf_op jit(solution)/shard_map/ppermute | solution.py:462
  110.5 8.1 %collective-permute-start.30 = (s16[528,256]{1,0:T(8,128)(2,1)S(1)}, s16[528,256]{1,0:T(8,128)(2,1)S(1)}, u32[]{:S(2)}, u32[]{:S(2)}) collective-permute-start(s16[528,256]{1,0:T(8,128)(2,1)S(1)} %get-tuple-element.79), channel_id=1, source_target_pairs={{0,16},{1,65},{2,18},{3,67},{4,20},{5,69},{6,22},{7,71},{8,24},{9,... | collective-permute-start | bytes 811016 | tf_op jit(solution)/shard_map/ppermute | solution.py:462
  112.2 9.2 %collective-permute-start.29 = (s16[528,256]{1,0:T(8,128)(2,1)S(1)}, s16[528,256]{1,0:T(8,128)(2,1)S(1)}, u32[]{:S(2)}, u32[]{:S(2)}) collective-permute-start(s16[528,256]{1,0:T(8,128)(2,1)S(1)} %get-tuple-element.79), channel_id=1, source_target_pairs={{0,24},{1,97},{2,26},{3,99},{4,28},{5,101},{6,30},{7,103},{8,16},{... | collective-permute-start | bytes 811016 | tf_op jit(solution)/shard_map/ppermute | solution.py:462
  115.1 6.5 %collective-permute-start.28 = (s16[528,256]{1,0:T(8,128)(2,1)S(1)}, s16[528,256]{1,0:T(8,128)(2,1)S(1)}, u32[]{:S(2)}, u32[]{:S(2)}) collective-permute-start(s16[528,256]{1,0:T(8,128)(2,1)S(1)} %get-tuple-element.79), channel_id=1, source_target_pairs={{0,8},{1,33},{2,10},{3,35},{4,12},{5,37},{6,14},{7,39},{8,0},{9,41... | collective-permute-start | bytes 811016 | tf_op jit(solution)/shard_map/ppermute | solution.py:462
  122.8 10.5 %collective-permute-start.33 = (bf16[512,256]{1,0:T(8,128)(2,1)S(1)}, bf16[512,256]{1,0:T(8,128)(2,1)S(1)}, u32[]{:S(2)}, u32[]{:S(2)}) collective-permute-start(bf16[512,256]{1,0:T(8,128)(2,1)S(1)} %get-tuple-element.82.a), channel_id=1, source_target_pairs={{0,96},{1,25},{2,98},{3,27},{4,100},{5,29},{6,102},{7,31},{8,104},... | collective-permute-start | bytes 786440 | tf_op jit(solution)/shard_map/ppermute | solution.py:462
  124.6 8.6 %collective-permute-start.32 = (bf16[512,256]{1,0:T(8,128)(2,1)S(1)}, bf16[512,256]{1,0:T(8,128)(2,1)S(1)}, u32[]{:S(2)}, u32[]{:S(2)}) collective-permute-start(bf16[512,256]{1,0:T(8,128)(2,1)S(1)} %get-tuple-element.82.a), channel_id=1, source_target_pairs={{0,64},{1,17},{2,66},{3,19},{4,68},{5,21},{6,70},{7,23},{8,72},{9,... | collective-permute-start | bytes 786440 | tf_op jit(solution)/shard_map/ppermute | solution.py:462
  125.4 8.7 %collective-permute-start.31 = (bf16[512,256]{1,0:T(8,128)(2,1)S(1)}, bf16[512,256]{1,0:T(8,128)(2,1)S(1)}, u32[]{:S(2)}, u32[]{:S(2)}) collective-permute-start(bf16[512,256]{1,0:T(8,128)(2,1)S(1)} %get-tuple-element.82.a), channel_id=1, source_target_pairs={{0,32},{1,9},{2,34},{3,11},{4,36},{5,13},{6,38},{7,15},{8,40},{9,1... | collective-permute-start | bytes 786440 | tf_op jit(solution)/shard_map/ppermute | solution.py:462
  158.0 12.4 %all-to-all-start = ((f32[16,24,128]{2,1,0:T(8,128)}), f32[16,24,128]{2,1,0:T(8,128)S(1)}, u32[]{:S(2)}, u32[]{:S(2)}) async-start(f32[16,24,128]{2,1,0:T(8,128)} %bitcast.34), calls=%async_computation | async-start | bytes 393216 | tf_op jit(solution)/shard_map/all_to_all | solution.py:608
  (36 other events, 332.7 us)
where the time goes:
time: 172 us
  waiting for transfers between devices  63.6 us (37%)
  starting transfers between devices  55.9 us (32%)
  Pallas kernels  36.9 us (21%)
  local copies, waits for them, and re-layouts  11.1 us (6%)
  other arithmetic  3.25 us (2%)
    ppermute x42, waiting for transfers between devices, send(): return lax.ppermute(value, ('row', 'col'), grid_pairs(move))  56.9 us
    ppermute x42, starting transfers between devices, send(): return lax.ppermute(value, ('row', 'col'), grid_pairs(move))  51.6 us
    pallas_call x22, Pallas kernels, call(): pl.pallas_call(kernel, out_shape=outs, in_specs=specs or [VMEM] * len(arg...  36.9 us
    unnamed x34, local copies, waits for them, and re-layouts  11 us
    all_to_all x1, waiting for transfers between devices, per_device(): gathered = lax.all_to_all(repeated, 'row', 0, 0, tiled=True)  6.72 us
    all_to_all x1, starting transfers between devices, per_device(): gathered = lax.all_to_all(repeated, 'row', 0, 0, tiled=True)  4.35 us
  transfers between devices with their start and end apart: 43, of which 33 were waited for; matrix products, arithmetic and copies ran while one was open for 2% of the time, Pallas kernels for 10%

commit v1 on v0

--- a/solution.py
+++ b/solution.py
@@ -274,9 +274,9 @@
     @pl.when(meta[M_OWNER] == 1)
     def _():
         for m in range(4):
-            for k in range(BAND):
-                slot = slot_of(meta, cols[start + m, k])
-                near[m] += nt(held[slot], tile_at(tiles, start + m, k))
+            chosen = [held[slot_of(meta, cols[start + m, k])] for k in range(BAND)]
+            band = [tile_at(tiles, start + m, k) for k in range(BAND)]
+            near[m] += nt(jnp.concatenate(chosen, axis=1), jnp.concatenate(band, axis=1))
 
     for m in (0, 2):
         s = start + m

time: 172 us -> 172 us (level)
  no operation moved by 1% of the time
where the time goes in v1:
time: 172 us
  waiting for transfers between devices  63.6 us (37%)
  starting transfers between devices  55.9 us (32%)
  Pallas kernels  36.9 us (21%)
  local copies, waits for them, and re-layouts  11.1 us (6%)
  other arithmetic  3.25 us (2%)
    ppermute x42, waiting for transfers between devices, send(): return lax.ppermute(value, ('row', 'col'), grid_pairs(move))  56.9 us
    ppermute x42, starting transfers between devices, send(): return lax.ppermute(value, ('row', 'col'), grid_pairs(move))  51.6 us
    pallas_call x22, Pallas kernels, call(): pl.pallas_call(kernel, out_shape=outs, in_specs=specs or [VMEM] * len(arg...  36.9 us
    unnamed x34, local copies, waits for them, and re-layouts  11 us
    all_to_all x1, waiting for transfers between devices, per_device(): gathered = lax.all_to_all(repeated, 'row', 0, 0, tiled=True)  6.72 us
    all_to_all x1, starting transfers between devices, per_device(): gathered = lax.all_to_all(repeated, 'row', 0, 0, tiled=True)  4.35 us
  transfers between devices with their start and end apart: 43, of which 33 were waited for; matrix products, arithmetic and copies ran while one was open for 2% of the time, Pallas kernels for 10%

profile of v1, /device:TPU:0, one launch (start us, length us, event | category | flops | bytes accessed | tf_op | source)
XLA Modules:
  0.0 171.8 jit_solution(5270054987666002079)
XLA Ops:
  3.6 3.2 %collective-permute-start.2 = (bf16[144,256]{1,0:T(8,128)(2,1)S(1)}, bf16[144,256]{1,0:T(8,128)(2,1)S(1)}, u32[]{:S(2)}, u32[]{:S(2)}) collective-permute-start(bf16[144,256]{1,0:T(8,128)(2,1)S(1)} %shard_map.94.a0), channel_id=1, source_target_pairs={{0,6},{1,7},{2,4},{3,5},{4,2},{5,3},{6,0},{7,1},{8,14},{9,15},{10,... | collective-permute-start | bytes 221192 | tf_op jit(solution)/shard_map/ppermute | solution.py:462
  16.6 3.4 %copy-done = bf16[1,1,128,128,256]{4,3,2,1,0:T(8,128)(2,1)S(1)} copy-done((bf16[1,1,128,128,256]{4,3,2,1,0:T(8,128)(2,1)S(1)}, bf16[1,1,128,128,256]{4,3,2,1,0:T(8,128)(2,1)}, u32[]{:S(2)}) %copy-start) | copy-done | bytes 8388632
  20.0 3.4 %copy-done.2 = bf16[1,1,128,128,256]{4,3,2,1,0:T(8,128)(2,1)S(1)} copy-done((bf16[1,1,128,128,256]{4,3,2,1,0:T(8,128)(2,1)S(1)}, bf16[1,1,128,128,256]{4,3,2,1,0:T(8,128)(2,1)}, u32[]{:S(2)}) %copy-start.2) | copy-done | bytes 8388632
  26.1 4.7 %shard_map.95 = (f32[16,128,256]{2,1,0:T(8,128)S(1)}, s32[8,128]{1,0:T(8,128)S(1)}) custom-call(s32[30]{0:T(128)S(1)} %stack.121.meta, f32[128,128]{1,0:T(8,128)S(1)} %fusion.live, bf16[128,128,256]{2,1,0:T(8,128)(2,1)S(1)} %bitcast.39, bf16[128,128,256]{2,1,0:T(8,128)(2,1)S(1)} %bitcast.48, bf16[144,256]{1,0:T(8,128)(2,1)S(1)} %shard_map.94.a0, ...), custom_call_target="tpu_custom_call" | custom-call | flops 4294967296 | bytes 65536 | tf_op jit(solution)/shard_map/pallas_call | solution.py:31
  35.4 3.1 %collective-permute-start.9 = (s16[528,256]{1,0:T(8,128)(2,1)S(1)}, s16[528,256]{1,0:T(8,128)(2,1)S(1)}, u32[]{:S(2)}, u32[]{:S(2)}) collective-permute-start(s16[528,256]{1,0:T(8,128)(2,1)S(1)} %get-tuple-element.57), channel_id=1, source_target_pairs={{0,96},{1,25},{2,98},{3,27},{4,100},{5,29},{6,102},{7,31},{8,104},... | collective-permute-start | bytes 811016 | tf_op jit(solution)/shard_map/ppermute | solution.py:462
  40.9 4.5 %collective-permute-done.9.g3 = s16[528,256]{1,0:T(8,128)(2,1)S(1)} collective-permute-done((s16[528,256]{1,0:T(8,128)(2,1)S(1)}, s16[528,256]{1,0:T(8,128)(2,1)S(1)}, u32[]{:S(2)}, u32[]{:S(2)}) %collective-permute-start.9) | collective-permute-done | bytes 270368 | tf_op jit(solution)/shard_map/ppermute | solution.py:462
  51.8 3.5 %collective-permute-done.13.p2 = s16[528,256]{1,0:T(8,128)(2,1)S(1)} collective-permute-done((s16[528,256]{1,0:T(8,128)(2,1)S(1)}, s16[528,256]{1,0:T(8,128)(2,1)S(1)}, u32[]{:S(2)}, u32[]{:S(2)}) %collective-permute-start.13) | collective-permute-done | bytes 270368 | tf_op jit(solution)/shard_map/ppermute | solution.py:462
  55.3 2.8 %collective-permute-done.12.p3 = s16[528,256]{1,0:T(8,128)(2,1)S(1)} collective-permute-done((s16[528,256]{1,0:T(8,128)(2,1)S(1)}, s16[528,256]{1,0:T(8,128)(2,1)S(1)}, u32[]{:S(2)}, u32[]{:S(2)}) %collective-permute-start.12) | collective-permute-done | bytes 270368 | tf_op jit(solution)/shard_map/ppermute | solution.py:462
  64.8 3.3 %collective-permute-done.16.b3 = bf16[512,256]{1,0:T(8,128)(2,1)S(1)} collective-permute-done((bf16[512,256]{1,0:T(8,128)(2,1)S(1)}, bf16[512,256]{1,0:T(8,128)(2,1)S(1)}, u32[]{:S(2)}, u32[]{:S(2)}) %collective-permute-start.16) | collective-permute-done | bytes 262176 | tf_op jit(solution)/shard_map/ppermute | solution.py:462
  70.1 3.2 %shard_map.101 = bf16[512,256]{1,0:T(8,128)(2,1)S(1)} custom-call(s32[30]{0:T(128)S(1)} %stack.121.meta, s32[8,128]{1,0:T(8,128)S(1)} %get-tuple-element.53.cols, f32[128,128]{1,0:T(8,128)S(1)} %fusion.live, bf16[128,128,256]{2,1,0:T(8,128)(2,1)S(1)} %bitcast.41, bf16[128,128,256]{2,1,0:T(8,128)(2,1)S(1)} %bitcast.50, f32[8,128,256]{2,1,0:T(8,128)S(1)} %shard_map.99.partial, ...), custom_call_target="tpu_custom_call" | custom-call | flops 1073741824 | bytes 65536 | tf_op jit(solution)/shard_map/pallas_call | solution.py:31
  73.4 3.1 %shard_map.100 = (f32[512,256]{1,0:T(8,128)S(1)}, f32[512,256]{1,0:T(8,128)S(1)}, f32[8,128]{1,0:T(8,128)S(1)}) custom-call(s32[30]{0:T(128)S(1)} %stack.121.meta, s32[8,128]{1,0:T(8,128)S(1)} %get-tuple-element.53.cols, f32[128,128]{1,0:T(8,128)S(1)} %fusion.live, bf16[128,128,256]{2,1,0:T(8,128)(2,1)S(1)} %bitcast.42, bf16[128,128,256]{2,1,0:T(8,128)(2,1)S(1)} %bitcast.51, ...), custom_call_target="tpu_custom_call" | custom-call | flops 1073741824 | bytes 65536 | tf_op jit(solution)/shard_map/pallas_call | solution.py:31
  78.1 2.7 %collective-permute-start.20 = (bf16[128,256]{1,0:T(8,128)(2,1)S(1)}, bf16[128,256]{1,0:T(8,128)(2,1)S(1)}, u32[]{:S(2)}, u32[]{:S(2)}) collective-permute-start(bf16[128,256]{1,0:T(8,128)(2,1)S(1)} %get-tuple-element.69), channel_id=1, source_target_pairs={{0,4},{1,5},{2,6},{3,7},{4,0},{5,1},{6,2},{7,3},{8,12},{9,13},{10,... | collective-permute-start | bytes 196616 | tf_op jit(solution)/shard_map/ppermute | solution.py:462
  93.6 4.9 %shard_map.104 = (s16[528,256]{1,0:T(8,128)(2,1)S(1)}, s16[528,256]{1,0:T(8,128)(2,1)S(1)}, s16[528,256]{1,0:T(8,128)(2,1)S(1)}, f32[16,128,256]{2,1,0:T(8,128)S...) custom-call(s32[30]{0:T(128)S(1)} %stack.121.meta, s32[8,128]{1,0:T(8,128)S(1)} %get-tuple-element.53.cols, ...), custom_call_target="tpu_custom_call" | custom-call | flops 1073741824 | bytes 65536 | tf_op jit(solution)/shard_map/pallas_call | solution.py:31
  105.0 3.0 %collective-permute-done.26.g3 = s16[528,256]{1,0:T(8,128)(2,1)S(1)} collective-permute-done((s16[528,256]{1,0:T(8,128)(2,1)S(1)}, s16[528,256]{1,0:T(8,128)(2,1)S(1)}, u32[]{:S(2)}, u32[]{:S(2)}) %collective-permute-start.26) | collective-permute-done | bytes 270368 | tf_op jit(solution)/shard_map/ppermute | solution.py:462
  112.2 2.9 %collective-permute-start.29 = (s16[528,256]{1,0:T(8,128)(2,1)S(1)}, s16[528,256]{1,0:T(8,128)(2,1)S(1)}, u32[]{:S(2)}, u32[]{:S(2)}) collective-permute-start(s16[528,256]{1,0:T(8,128)(2,1)S(1)} %get-tuple-element.79), channel_id=1, source_target_pairs={{0,24},{1,97},{2,26},{3,99},{4,28},{5,101},{6,30},{7,103},{8,16},{... | collective-permute-start | bytes 811016 | tf_op jit(solution)/shard_map/ppermute | solution.py:462
  115.1 3.6 %collective-permute-done.30.p2 = s16[528,256]{1,0:T(8,128)(2,1)S(1)} collective-permute-done((s16[528,256]{1,0:T(8,128)(2,1)S(1)}, s16[528,256]{1,0:T(8,128)(2,1)S(1)}, u32[]{:S(2)}, u32[]{:S(2)}) %collective-permute-start.30) | collective-permute-done | bytes 270368 | tf_op jit(solution)/shard_map/ppermute | solution.py:462
  118.6 2.8 %collective-permute-done.29.p3 = s16[528,256]{1,0:T(8,128)(2,1)S(1)} collective-permute-done((s16[528,256]{1,0:T(8,128)(2,1)S(1)}, s16[528,256]{1,0:T(8,128)(2,1)S(1)}, u32[]{:S(2)}, u32[]{:S(2)}) %collective-permute-start.29) | collective-permute-done | bytes 270368 | tf_op jit(solution)/shard_map/ppermute | solution.py:462
  128.8 4.4 %collective-permute-done.33.b3 = bf16[512,256]{1,0:T(8,128)(2,1)S(1)} collective-permute-done((bf16[512,256]{1,0:T(8,128)(2,1)S(1)}, bf16[512,256]{1,0:T(8,128)(2,1)S(1)}, u32[]{:S(2)}, u32[]{:S(2)}) %collective-permute-start.33) | collective-permute-done | bytes 262176 | tf_op jit(solution)/shard_map/ppermute | solution.py:462
  134.2 3.0 %shard_map.110 = bf16[512,256]{1,0:T(8,128)(2,1)S(1)} custom-call(s32[30]{0:T(128)S(1)} %stack.121.meta, s32[8,128]{1,0:T(8,128)S(1)} %get-tuple-element.53.cols, f32[128,128]{1,0:T(8,128)S(1)} %fusion.live, bf16[128,128,256]{2,1,0:T(8,128)(2,1)S(1)} %bitcast.46, bf16[128,128,256]{2,1,0:T(8,128)(2,1)S(1)} %bitcast.55, ...), custom_call_target="tpu_custom_call" | custom-call | flops 1073741824 | bytes 65536 | tf_op jit(solution)/shard_map/pallas_call | solution.py:31
  137.3 3.1 %shard_map.109 = (f32[512,256]{1,0:T(8,128)S(1)}, f32[512,256]{1,0:T(8,128)S(1)}, f32[8,128]{1,0:T(8,128)S(1)}) custom-call(s32[30]{0:T(128)S(1)} %stack.121.meta, s32[8,128]{1,0:T(8,128)S(1)} %get-tuple-element.53.cols, f32[128,128]{1,0:T(8,128)S(1)} %fusion.live, bf16[128,128,256]{2,1,0:T(8,128)(2,1)S(1)} %bitcast.47, bf16[128,128,256]{2,1,0:T(8,128)(2,1)S(1)} %bitcast.56, ...), custom_call_target="tpu_custom_call" | custom-call | flops 1073741824 | bytes 65536 | tf_op jit(solution)/shard_map/pallas_call | solution.py:31
  141.9 2.8 %collective-permute-start.37 = (bf16[128,256]{1,0:T(8,128)(2,1)S(1)}, bf16[128,256]{1,0:T(8,128)(2,1)S(1)}, u32[]{:S(2)}, u32[]{:S(2)}) collective-permute-start(bf16[128,256]{1,0:T(8,128)(2,1)S(1)} %get-tuple-element.91), channel_id=1, source_target_pairs={{0,4},{1,5},{2,6},{3,7},{4,0},{5,1},{6,2},{7,3},{8,12},{9,13},{10,... | collective-permute-start | bytes 196616 | tf_op jit(solution)/shard_map/ppermute | solution.py:462
  149.6 2.8 %collective-permute-start.41 = (f32[24,128]{1,0:T(8,128)S(1)}, f32[24,128]{1,0:T(8,128)S(1)}, u32[]{:S(2)}, u32[]{:S(2)}) collective-permute-start(f32[24,128]{1,0:T(8,128)S(1)} %add.45.own), channel_id=1, source_target_pairs={{0,4},{1,5},{2,6},{3,7},{4,0},{5,1},{6,2},{7,3},{8,12},{9,13},{10,... | collective-permute-start | bytes 36872 | tf_op jit(solution)/shard_map/ppermute | solution.py:462
  158.0 4.4 %all-to-all-start = ((f32[16,24,128]{2,1,0:T(8,128)}), f32[16,24,128]{2,1,0:T(8,128)S(1)}, u32[]{:S(2)}, u32[]{:S(2)}) async-start(f32[16,24,128]{2,1,0:T(8,128)} %bitcast.34), calls=%async_computation | async-start | bytes 393216 | tf_op jit(solution)/shard_map/all_to_all | solution.py:608
  163.7 6.7 %all-to-all-done = f32[16,24,128]{2,1,0:T(8,128)S(1)} async-done(((f32[16,24,128]{2,1,0:T(8,128)}), f32[16,24,128]{2,1,0:T(8,128)S(1)}, u32[]{:S(2)}, u32[]{:S(2)}) %all-to-all-start) | async-done | bytes 196640 | tf_op jit(solution)/shard_map/all_to_all | solution.py:608
  (126 shorter events, 85.6 us)
Async XLA Ops:
  0.6 7.2 %collective-permute-start.4 = (bf16[3,256,256]{2,1,0:T(8,128)(2,1)}, bf16[3,256,256]{2,1,0:T(8,128)(2,1)S(1)}, u32[]{:S(2)}, u32[]{:S(2)}) collective-permute-start(bf16[3,256,256]{2,1,0:T(8,128)(2,1)} %bitcast.65), channel_id=1, source_target_pairs={{1,0},{3,2},{5,4},{7,6},{9,8},{11,10},{13,12},{15,14},{16,17},{18,... | collective-permute-start | bytes 1179656 | tf_op jit(solution)/shard_map/ppermute | solution.py:462
  3.6 7.8 %collective-permute-start.2 = (bf16[144,256]{1,0:T(8,128)(2,1)S(1)}, bf16[144,256]{1,0:T(8,128)(2,1)S(1)}, u32[]{:S(2)}, u32[]{:S(2)}) collective-permute-start(bf16[144,256]{1,0:T(8,128)(2,1)S(1)} %shard_map.94.a0), channel_id=1, source_target_pairs={{0,6},{1,7},{2,4},{3,5},{4,2},{5,3},{6,0},{7,1},{8,14},{9,15},{10,... | collective-permute-start | bytes 221192 | tf_op jit(solution)/shard_map/ppermute | solution.py:462
  6.8 6.6 %collective-permute-start.1 = (bf16[144,256]{1,0:T(8,128)(2,1)S(1)}, bf16[144,256]{1,0:T(8,128)(2,1)S(1)}, u32[]{:S(2)}, u32[]{:S(2)}) collective-permute-start(bf16[144,256]{1,0:T(8,128)(2,1)S(1)} %shard_map.94.a0), channel_id=1, source_target_pairs={{0,4},{1,5},{2,6},{3,7},{4,0},{5,1},{6,2},{7,3},{8,12},{9,13},{10,... | collective-permute-start | bytes 221192 | tf_op jit(solution)/shard_map/ppermute | solution.py:462
  8.9 23.5 %collective-permute-start.7 = (bf16[6,256,256]{2,1,0:T(8,128)(2,1)S(1)}, bf16[6,256,256]{2,1,0:T(8,128)(2,1)S(1)}, u32[]{:S(2)}, u32[]{:S(2)}) collective-permute-start(bf16[6,256,256]{2,1,0:T(8,128)(2,1)S(1)} %pad_maximum_fusion.t0), channel_id=1, source_target_pairs={{6,0},{14,8},{23,17},{31,25},{36,34},{44,42},{53,51},{61,59},{66,6... | collective-permute-start | bytes 2359304 | tf_op jit(solution)/shard_map/ppermute | solution.py:462
  10.2 22.2 %collective-permute-start.6 = (bf16[6,256,256]{2,1,0:T(8,128)(2,1)S(1)}, bf16[6,256,256]{2,1,0:T(8,128)(2,1)S(1)}, u32[]{:S(2)}, u32[]{:S(2)}) collective-permute-start(bf16[6,256,256]{2,1,0:T(8,128)(2,1)S(1)} %pad_maximum_fusion.t0), channel_id=1, source_target_pairs={{4,0},{12,8},{21,17},{29,25},{38,34},{46,42},{55,51},{63,59},{64,6... | collective-permute-start | bytes 2359304 | tf_op jit(solution)/shard_map/ppermute | solution.py:462
  11.5 20.9 %collective-permute-start.5 = (bf16[6,256,256]{2,1,0:T(8,128)(2,1)S(1)}, bf16[6,256,256]{2,1,0:T(8,128)(2,1)S(1)}, u32[]{:S(2)}, u32[]{:S(2)}) collective-permute-start(bf16[6,256,256]{2,1,0:T(8,128)(2,1)S(1)} %pad_maximum_fusion.t0), channel_id=1, source_target_pairs={{2,0},{10,8},{19,17},{27,25},{32,34},{40,42},{49,51},{57,59},{70,6... | collective-permute-start | bytes 2359304 | tf_op jit(solution)/shard_map/ppermute | solution.py:462
  34.4 6.5 %collective-permute-start.8 = (s16[528,256]{1,0:T(8,128)(2,1)S(1)}, s16[528,256]{1,0:T(8,128)(2,1)S(1)}, u32[]{:S(2)}, u32[]{:S(2)}) collective-permute-start(s16[528,256]{1,0:T(8,128)(2,1)S(1)} %get-tuple-element.56), channel_id=1, source_target_pairs={{0,32},{1,9},{2,34},{3,11},{4,36},{5,13},{6,38},{7,15},{8,40},{9,1... | collective-permute-start | bytes 811016 | tf_op jit(solution)/shard_map/ppermute | solution.py:462
  35.4 10.0 %collective-permute-start.9 = (s16[528,256]{1,0:T(8,128)(2,1)S(1)}, s16[528,256]{1,0:T(8,128)(2,1)S(1)}, u32[]{:S(2)}, u32[]{:S(2)}) collective-permute-start(s16[528,256]{1,0:T(8,128)(2,1)S(1)} %get-tuple-element.57), channel_id=1, source_target_pairs={{0,96},{1,25},{2,98},{3,27},{4,100},{5,29},{6,102},{7,31},{8,104},... | collective-permute-start | bytes 811016 | tf_op jit(solution)/shard_map/ppermute | solution.py:462
  38.5 8.0 %collective-permute-start.10 = (s16[528,256]{1,0:T(8,128)(2,1)S(1)}, s16[528,256]{1,0:T(8,128)(2,1)S(1)}, u32[]{:S(2)}, u32[]{:S(2)}) collective-permute-start(s16[528,256]{1,0:T(8,128)(2,1)S(1)} %get-tuple-element.58), channel_id=1, source_target_pairs={{0,64},{1,17},{2,66},{3,19},{4,68},{5,21},{6,70},{7,23},{8,72},{9,... | collective-permute-start | bytes 811016 | tf_op jit(solution)/shard_map/ppermute | solution.py:462
  47.2 8.1 %collective-permute-start.13 = (s16[528,256]{1,0:T(8,128)(2,1)S(1)}, s16[528,256]{1,0:T(8,128)(2,1)S(1)}, u32[]{:S(2)}, u32[]{:S(2)}) collective-permute-start(s16[528,256]{1,0:T(8,128)(2,1)S(1)} %get-tuple-element.60), channel_id=1, source_target_pairs={{0,16},{1,65},{2,18},{3,67},{4,20},{5,69},{6,22},{7,71},{8,24},{9,... | collective-permute-start | bytes 811016 | tf_op jit(solution)/shard_map/ppermute | solution.py:462
  49.4 8.7 %collective-permute-start.12 = (s16[528,256]{1,0:T(8,128)(2,1)S(1)}, s16[528,256]{1,0:T(8,128)(2,1)S(1)}, u32[]{:S(2)}, u32[]{:S(2)}) collective-permute-start(s16[528,256]{1,0:T(8,128)(2,1)S(1)} %get-tuple-element.60), channel_id=1, source_target_pairs={{0,24},{1,97},{2,26},{3,99},{4,28},{5,101},{6,30},{7,103},{8,16},{... | collective-permute-start | bytes 811016 | tf_op jit(solution)/shard_map/ppermute | solution.py:462
  58.7 9.4 %collective-permute-start.16 = (bf16[512,256]{1,0:T(8,128)(2,1)S(1)}, bf16[512,256]{1,0:T(8,128)(2,1)S(1)}, u32[]{:S(2)}, u32[]{:S(2)}) collective-permute-start(bf16[512,256]{1,0:T(8,128)(2,1)S(1)} %get-tuple-element.62.a), channel_id=1, source_target_pairs={{0,96},{1,25},{2,98},{3,27},{4,100},{5,29},{6,102},{7,31},{8,104},... | collective-permute-start | bytes 786440 | tf_op jit(solution)/shard_map/ppermute | solution.py:462
  61.4 7.9 %collective-permute-start.15 = (bf16[512,256]{1,0:T(8,128)(2,1)S(1)}, bf16[512,256]{1,0:T(8,128)(2,1)S(1)}, u32[]{:S(2)}, u32[]{:S(2)}) collective-permute-start(bf16[512,256]{1,0:T(8,128)(2,1)S(1)} %get-tuple-element.62.a), channel_id=1, source_target_pairs={{0,64},{1,17},{2,66},{3,19},{4,68},{5,21},{6,70},{7,23},{8,72},{9,... | collective-permute-start | bytes 786440 | tf_op jit(solution)/shard_map/ppermute | solution.py:462
  61.4 8.7 %collective-permute-start.14 = (bf16[512,256]{1,0:T(8,128)(2,1)S(1)}, bf16[512,256]{1,0:T(8,128)(2,1)S(1)}, u32[]{:S(2)}, u32[]{:S(2)}) collective-permute-start(bf16[512,256]{1,0:T(8,128)(2,1)S(1)} %get-tuple-element.62.a), channel_id=1, source_target_pairs={{0,32},{1,9},{2,34},{3,11},{4,36},{5,13},{6,38},{7,15},{8,40},{9,1... | collective-permute-start | bytes 786440 | tf_op jit(solution)/shard_map/ppermute | solution.py:462
  98.5 6.5 %collective-permute-start.25 = (s16[528,256]{1,0:T(8,128)(2,1)S(1)}, s16[528,256]{1,0:T(8,128)(2,1)S(1)}, u32[]{:S(2)}, u32[]{:S(2)}) collective-permute-start(s16[528,256]{1,0:T(8,128)(2,1)S(1)} %get-tuple-element.74), channel_id=1, source_target_pairs={{0,32},{1,9},{2,34},{3,11},{4,36},{5,13},{6,38},{7,15},{8,40},{9,1... | collective-permute-start | bytes 811016 | tf_op jit(solution)/shard_map/ppermute | solution.py:462
  99.1 8.9 %collective-permute-start.26 = (s16[528,256]{1,0:T(8,128)(2,1)S(1)}, s16[528,256]{1,0:T(8,128)(2,1)S(1)}, u32[]{:S(2)}, u32[]{:S(2)}) collective-permute-start(s16[528,256]{1,0:T(8,128)(2,1)S(1)} %get-tuple-element.75), channel_id=1, source_target_pairs={{0,96},{1,25},{2,98},{3,27},{4,100},{5,29},{6,102},{7,31},{8,104},... | collective-permute-start | bytes 811016 | tf_op jit(solution)/shard_map/ppermute | solution.py:462
  101.1 8.7 %collective-permute-start.27 = (s16[528,256]{1,0:T(8,128)(2,1)S(1)}, s16[528,256]{1,0:T(8,128)(2,1)S(1)}, u32[]{:S(2)}, u32[]{:S(2)}) collective-permute-start(s16[528,256]{1,0:T(8,128)(2,1)S(1)} %get-tuple-element.76), channel_id=1, source_target_pairs={{0,64},{1,17},{2,66},{3,19},{4,68},{5,21},{6,70},{7,23},{8,72},{9,... | collective-permute-start | bytes 811016 | tf_op jit(solution)/shard_map/ppermute | solution.py:462
  110.5 8.1 %collective-permute-start.30 = (s16[528,256]{1,0:T(8,128)(2,1)S(1)}, s16[528,256]{1,0:T(8,128)(2,1)S(1)}, u32[]{:S(2)}, u32[]{:S(2)}) collective-permute-start(s16[528,256]{1,0:T(8,128)(2,1)S(1)} %get-tuple-element.79), channel_id=1, source_target_pairs={{0,16},{1,65},{2,18},{3,67},{4,20},{5,69},{6,22},{7,71},{8,24},{9,... | collective-permute-start | bytes 811016 | tf_op jit(solution)/shard_map/ppermute | solution.py:462
  112.2 9.2 %collective-permute-start.29 = (s16[528,256]{1,0:T(8,128)(2,1)S(1)}, s16[528,256]{1,0:T(8,128)(2,1)S(1)}, u32[]{:S(2)}, u32[]{:S(2)}) collective-permute-start(s16[528,256]{1,0:T(8,128)(2,1)S(1)} %get-tuple-element.79), channel_id=1, source_target_pairs={{0,24},{1,97},{2,26},{3,99},{4,28},{5,101},{6,30},{7,103},{8,16},{... | collective-permute-start | bytes 811016 | tf_op jit(solution)/shard_map/ppermute | solution.py:462
  115.1 6.5 %collective-permute-start.28 = (s16[528,256]{1,0:T(8,128)(2,1)S(1)}, s16[528,256]{1,0:T(8,128)(2,1)S(1)}, u32[]{:S(2)}, u32[]{:S(2)}) collective-permute-start(s16[528,256]{1,0:T(8,128)(2,1)S(1)} %get-tuple-element.79), channel_id=1, source_target_pairs={{0,8},{1,33},{2,10},{3,35},{4,12},{5,37},{6,14},{7,39},{8,0},{9,41... | collective-permute-start | bytes 811016 | tf_op jit(solution)/shard_map/ppermute | solution.py:462
  122.8 10.5 %collective-permute-start.33 = (bf16[512,256]{1,0:T(8,128)(2,1)S(1)}, bf16[512,256]{1,0:T(8,128)(2,1)S(1)}, u32[]{:S(2)}, u32[]{:S(2)}) collective-permute-start(bf16[512,256]{1,0:T(8,128)(2,1)S(1)} %get-tuple-element.82.a), channel_id=1, source_target_pairs={{0,96},{1,25},{2,98},{3,27},{4,100},{5,29},{6,102},{7,31},{8,104},... | collective-permute-start | bytes 786440 | tf_op jit(solution)/shard_map/ppermute | solution.py:462
  124.6 8.6 %collective-permute-start.32 = (bf16[512,256]{1,0:T(8,128)(2,1)S(1)}, bf16[512,256]{1,0:T(8,128)(2,1)S(1)}, u32[]{:S(2)}, u32[]{:S(2)}) collective-permute-start(bf16[512,256]{1,0:T(8,128)(2,1)S(1)} %get-tuple-element.82.a), channel_id=1, source_target_pairs={{0,64},{1,17},{2,66},{3,19},{4,68},{5,21},{6,70},{7,23},{8,72},{9,... | collective-permute-start | bytes 786440 | tf_op jit(solution)/shard_map/ppermute | solution.py:462
  125.4 8.7 %collective-permute-start.31 = (bf16[512,256]{1,0:T(8,128)(2,1)S(1)}, bf16[512,256]{1,0:T(8,128)(2,1)S(1)}, u32[]{:S(2)}, u32[]{:S(2)}) collective-permute-start(bf16[512,256]{1,0:T(8,128)(2,1)S(1)} %get-tuple-element.82.a), channel_id=1, source_target_pairs={{0,32},{1,9},{2,34},{3,11},{4,36},{5,13},{6,38},{7,15},{8,40},{9,1... | collective-permute-start | bytes 786440 | tf_op jit(solution)/shard_map/ppermute | solution.py:462
  158.0 12.4 %all-to-all-start = ((f32[16,24,128]{2,1,0:T(8,128)}), f32[16,24,128]{2,1,0:T(8,128)S(1)}, u32[]{:S(2)}, u32[]{:S(2)}) async-start(f32[16,24,128]{2,1,0:T(8,128)} %bitcast.34), calls=%async_computation | async-start | bytes 393216 | tf_op jit(solution)/shard_map/all_to_all | solution.py:608
  (36 other events, 332.7 us)

commit v2 on v0

--- a/solution.py
+++ b/solution.py
@@ -300,7 +300,7 @@
         meta, cols, live, left, right, partial, (a, b1, b2, b3), (t0, t1, t2, t3), out, near, held, 0
     )
     lane = lax.broadcasted_iota(jnp.int32, (RHS, LEAF), 1)
-    for m in range(4):
+    for m in range(own.shape[0] // RHS):
         rows = slice(m * RHS, (m + 1) * RHS)
         vector, j = own[rows], meta[m]
         before = held[slot_of(meta, (j + ROWS - 1) % ROWS)][:, LEAF - RHS :].astype(F32)[:, RHS - 1 :]
@@ -367,9 +367,10 @@
     for m, total in enumerate(group_totals(own, p1, p3, p2)):
         rows = slice(m * RHS, (m + 1) * RHS)
         whole = without_rims(curved[rows], before, after, meta[m])
-        curved_out[rows] = whole
         vector = first[rows] - step * (total + weight * whole)
-        full[rows] = vector
+        if m == 0:
+            curved_out[...] = whole
+            full[...] = vector
         sent[rows] = vector.astype(BF16)
 
 
@@ -563,7 +564,7 @@
         )
         other = send(parts, core_move)
         own, curved, edges = call(
-            forward_second_kernel, (group4, group4, sums_shape), meta, cols, *factors(), partial, *pieces, *tiles, vector,
+            forward_second_kernel, (group4, shape(vector.shape), sums_shape), meta, cols, *factors(), partial, *pieces, *tiles, vector,
             specs=specs(2, 13), scratch=scratch, flops=1 << 30,
         )
         own, p1, p3, p2 = call(core_phase_kernel, (vec, sent_shape, sent_shape, sent_shape), own, other)
@@ -595,7 +596,7 @@
     )
     own, sums, parts = sum_over_row(own, sums, (g1, g3, g2))
     s2, s2_sent, d1, sums1 = call(
-        descent2_kernel, (group4, group4_sent, group4, sums_shape), meta, reg, s1, d1, rims, own, sums, *parts,
+        descent2_kernel, (vec, group4_sent, vec, sums_shape), meta, reg, s1, d1, rims, own, sums, *parts,
         specs=specs(1, 9),
     )
     d2, edges, parts = product(s2, s2_sent)

time: 172 us -> 172 us (level)
  no operation moved by 1% of the time
where the time goes in v2:
time: 172 us
  waiting for transfers between devices  63.6 us (37%)
  starting transfers between devices  55.9 us (32%)
  Pallas kernels  36.8 us (21%)
  local copies, waits for them, and re-layouts  11.1 us (6%)
  other arithmetic  3.25 us (2%)
    ppermute x42, waiting for transfers between devices, send(): return lax.ppermute(value, ('row', 'col'), grid_pairs(move))  56.9 us
    ppermute x42, starting transfers between devices, send(): return lax.ppermute(value, ('row', 'col'), grid_pairs(move))  51.6 us
    pallas_call x22, Pallas kernels, call(): pl.pallas_call(kernel, out_shape=outs, in_specs=specs or [VMEM] * len(arg...  36.8 us
    unnamed x34, local copies, waits for them, and re-layouts  11 us
    all_to_all x1, waiting for transfers between devices, per_device(): gathered = lax.all_to_all(repeated, 'row', 0, 0, tiled=True)  6.72 us
    all_to_all x1, starting transfers between devices, per_device(): gathered = lax.all_to_all(repeated, 'row', 0, 0, tiled=True)  4.33 us
  transfers between devices with their start and end apart: 43, of which 33 were waited for; matrix products, arithmetic and copies ran while one was open for 2% of the time, Pallas kernels for 10%

profile of v2, /device:TPU:0, one launch (start us, length us, event | category | flops | bytes accessed | tf_op | source)
XLA Modules:
  0.0 171.7 jit_solution(658774306269586787)
XLA Ops:
  3.6 3.2 %collective-permute-start.2 = (bf16[144,256]{1,0:T(8,128)(2,1)S(1)}, bf16[144,256]{1,0:T(8,128)(2,1)S(1)}, u32[]{:S(2)}, u32[]{:S(2)}) collective-permute-start(bf16[144,256]{1,0:T(8,128)(2,1)S(1)} %shard_map.94.a0), channel_id=1, source_target_pairs={{0,6},{1,7},{2,4},{3,5},{4,2},{5,3},{6,0},{7,1},{8,14},{9,15},{10,... | collective-permute-start | bytes 221192 | tf_op jit(solution)/shard_map/ppermute | solution.py:463
  16.6 3.4 %copy-done = bf16[1,1,128,128,256]{4,3,2,1,0:T(8,128)(2,1)S(1)} copy-done((bf16[1,1,128,128,256]{4,3,2,1,0:T(8,128)(2,1)S(1)}, bf16[1,1,128,128,256]{4,3,2,1,0:T(8,128)(2,1)}, u32[]{:S(2)}) %copy-start) | copy-done | bytes 8388632
  20.0 3.4 %copy-done.2 = bf16[1,1,128,128,256]{4,3,2,1,0:T(8,128)(2,1)S(1)} copy-done((bf16[1,1,128,128,256]{4,3,2,1,0:T(8,128)(2,1)S(1)}, bf16[1,1,128,128,256]{4,3,2,1,0:T(8,128)(2,1)}, u32[]{:S(2)}) %copy-start.2) | copy-done | bytes 8388632
  26.1 4.7 %shard_map.95 = (f32[16,128,256]{2,1,0:T(8,128)S(1)}, s32[8,128]{1,0:T(8,128)S(1)}) custom-call(s32[30]{0:T(128)S(1)} %stack.121.meta, f32[128,128]{1,0:T(8,128)S(1)} %fusion.live, bf16[128,128,256]{2,1,0:T(8,128)(2,1)S(1)} %bitcast.39, bf16[128,128,256]{2,1,0:T(8,128)(2,1)S(1)} %bitcast.48, bf16[144,256]{1,0:T(8,128)(2,1)S(1)} %shard_map.94.a0, ...), custom_call_target="tpu_custom_call" | custom-call | flops 4294967296 | bytes 65536 | tf_op jit(solution)/shard_map/pallas_call | solution.py:31
  35.4 3.1 %collective-permute-start.9 = (s16[528,256]{1,0:T(8,128)(2,1)S(1)}, s16[528,256]{1,0:T(8,128)(2,1)S(1)}, u32[]{:S(2)}, u32[]{:S(2)}) collective-permute-start(s16[528,256]{1,0:T(8,128)(2,1)S(1)} %get-tuple-element.57), channel_id=1, source_target_pairs={{0,96},{1,25},{2,98},{3,27},{4,100},{5,29},{6,102},{7,31},{8,104},... | collective-permute-start | bytes 811016 | tf_op jit(solution)/shard_map/ppermute | solution.py:463
  40.9 4.5 %collective-permute-done.9.g3 = s16[528,256]{1,0:T(8,128)(2,1)S(1)} collective-permute-done((s16[528,256]{1,0:T(8,128)(2,1)S(1)}, s16[528,256]{1,0:T(8,128)(2,1)S(1)}, u32[]{:S(2)}, u32[]{:S(2)}) %collective-permute-start.9) | collective-permute-done | bytes 270368 | tf_op jit(solution)/shard_map/ppermute | solution.py:463
  51.8 3.5 %collective-permute-done.13.p2 = s16[528,256]{1,0:T(8,128)(2,1)S(1)} collective-permute-done((s16[528,256]{1,0:T(8,128)(2,1)S(1)}, s16[528,256]{1,0:T(8,128)(2,1)S(1)}, u32[]{:S(2)}, u32[]{:S(2)}) %collective-permute-start.13) | collective-permute-done | bytes 270368 | tf_op jit(solution)/shard_map/ppermute | solution.py:463
  55.3 2.8 %collective-permute-done.12.p3 = s16[528,256]{1,0:T(8,128)(2,1)S(1)} collective-permute-done((s16[528,256]{1,0:T(8,128)(2,1)S(1)}, s16[528,256]{1,0:T(8,128)(2,1)S(1)}, u32[]{:S(2)}, u32[]{:S(2)}) %collective-permute-start.12) | collective-permute-done | bytes 270368 | tf_op jit(solution)/shard_map/ppermute | solution.py:463
  64.8 3.3 %collective-permute-done.16.b3 = bf16[512,256]{1,0:T(8,128)(2,1)S(1)} collective-permute-done((bf16[512,256]{1,0:T(8,128)(2,1)S(1)}, bf16[512,256]{1,0:T(8,128)(2,1)S(1)}, u32[]{:S(2)}, u32[]{:S(2)}) %collective-permute-start.16) | collective-permute-done | bytes 262176 | tf_op jit(solution)/shard_map/ppermute | solution.py:463
  70.1 3.2 %shard_map.101 = bf16[512,256]{1,0:T(8,128)(2,1)S(1)} custom-call(s32[30]{0:T(128)S(1)} %stack.121.meta, s32[8,128]{1,0:T(8,128)S(1)} %get-tuple-element.53.cols, f32[128,128]{1,0:T(8,128)S(1)} %fusion.live, bf16[128,128,256]{2,1,0:T(8,128)(2,1)S(1)} %bitcast.41, bf16[128,128,256]{2,1,0:T(8,128)(2,1)S(1)} %bitcast.50, f32[8,128,256]{2,1,0:T(8,128)S(1)} %shard_map.99.partial, ...), custom_call_target="tpu_custom_call" | custom-call | flops 1073741824 | bytes 65536 | tf_op jit(solution)/shard_map/pallas_call | solution.py:31
  73.4 3.1 %shard_map.100 = (f32[512,256]{1,0:T(8,128)S(1)}, f32[512,256]{1,0:T(8,128)S(1)}, f32[8,128]{1,0:T(8,128)S(1)}) custom-call(s32[30]{0:T(128)S(1)} %stack.121.meta, s32[8,128]{1,0:T(8,128)S(1)} %get-tuple-element.53.cols, f32[128,128]{1,0:T(8,128)S(1)} %fusion.live, bf16[128,128,256]{2,1,0:T(8,128)(2,1)S(1)} %bitcast.42, bf16[128,128,256]{2,1,0:T(8,128)(2,1)S(1)} %bitcast.51, ...), custom_call_target="tpu_custom_call" | custom-call | flops 1073741824 | bytes 65536 | tf_op jit(solution)/shard_map/pallas_call | solution.py:31
  78.1 2.7 %collective-permute-start.20 = (bf16[128,256]{1,0:T(8,128)(2,1)S(1)}, bf16[128,256]{1,0:T(8,128)(2,1)S(1)}, u32[]{:S(2)}, u32[]{:S(2)}) collective-permute-start(bf16[128,256]{1,0:T(8,128)(2,1)S(1)} %get-tuple-element.69), channel_id=1, source_target_pairs={{0,4},{1,5},{2,6},{3,7},{4,0},{5,1},{6,2},{7,3},{8,12},{9,13},{10,... | collective-permute-start | bytes 196616 | tf_op jit(solution)/shard_map/ppermute | solution.py:463
  93.6 4.9 %shard_map.104 = (s16[528,256]{1,0:T(8,128)(2,1)S(1)}, s16[528,256]{1,0:T(8,128)(2,1)S(1)}, s16[528,256]{1,0:T(8,128)(2,1)S(1)}, f32[16,128,256]{2,1,0:T(8,128)S...) custom-call(s32[30]{0:T(128)S(1)} %stack.121.meta, s32[8,128]{1,0:T(8,128)S(1)} %get-tuple-element.53.cols, ...), custom_call_target="tpu_custom_call" | custom-call | flops 1073741824 | bytes 65536 | tf_op jit(solution)/shard_map/pallas_call | solution.py:31
  105.0 3.0 %collective-permute-done.26.g3 = s16[528,256]{1,0:T(8,128)(2,1)S(1)} collective-permute-done((s16[528,256]{1,0:T(8,128)(2,1)S(1)}, s16[528,256]{1,0:T(8,128)(2,1)S(1)}, u32[]{:S(2)}, u32[]{:S(2)}) %collective-permute-start.26) | collective-permute-done | bytes 270368 | tf_op jit(solution)/shard_map/ppermute | solution.py:463
  112.2 2.9 %collective-permute-start.29 = (s16[528,256]{1,0:T(8,128)(2,1)S(1)}, s16[528,256]{1,0:T(8,128)(2,1)S(1)}, u32[]{:S(2)}, u32[]{:S(2)}) collective-permute-start(s16[528,256]{1,0:T(8,128)(2,1)S(1)} %get-tuple-element.79), channel_id=1, source_target_pairs={{0,24},{1,97},{2,26},{3,99},{4,28},{5,101},{6,30},{7,103},{8,16},{... | collective-permute-start | bytes 811016 | tf_op jit(solution)/shard_map/ppermute | solution.py:463
  115.1 3.5 %collective-permute-done.30.p2 = s16[528,256]{1,0:T(8,128)(2,1)S(1)} collective-permute-done((s16[528,256]{1,0:T(8,128)(2,1)S(1)}, s16[528,256]{1,0:T(8,128)(2,1)S(1)}, u32[]{:S(2)}, u32[]{:S(2)}) %collective-permute-start.30) | collective-permute-done | bytes 270368 | tf_op jit(solution)/shard_map/ppermute | solution.py:463
  118.6 2.8 %collective-permute-done.29.p3 = s16[528,256]{1,0:T(8,128)(2,1)S(1)} collective-permute-done((s16[528,256]{1,0:T(8,128)(2,1)S(1)}, s16[528,256]{1,0:T(8,128)(2,1)S(1)}, u32[]{:S(2)}, u32[]{:S(2)}) %collective-permute-start.29) | collective-permute-done | bytes 270368 | tf_op jit(solution)/shard_map/ppermute | solution.py:463
  128.8 4.4 %collective-permute-done.33.b3 = bf16[512,256]{1,0:T(8,128)(2,1)S(1)} collective-permute-done((bf16[512,256]{1,0:T(8,128)(2,1)S(1)}, bf16[512,256]{1,0:T(8,128)(2,1)S(1)}, u32[]{:S(2)}, u32[]{:S(2)}) %collective-permute-start.33) | collective-permute-done | bytes 262176 | tf_op jit(solution)/shard_map/ppermute | solution.py:463
  134.2 3.0 %shard_map.110 = bf16[512,256]{1,0:T(8,128)(2,1)S(1)} custom-call(s32[30]{0:T(128)S(1)} %stack.121.meta, s32[8,128]{1,0:T(8,128)S(1)} %get-tuple-element.53.cols, f32[128,128]{1,0:T(8,128)S(1)} %fusion.live, bf16[128,128,256]{2,1,0:T(8,128)(2,1)S(1)} %bitcast.46, bf16[128,128,256]{2,1,0:T(8,128)(2,1)S(1)} %bitcast.55, ...), custom_call_target="tpu_custom_call" | custom-call | flops 1073741824 | bytes 65536 | tf_op jit(solution)/shard_map/pallas_call | solution.py:31
  137.3 3.1 %shard_map.109 = (f32[512,256]{1,0:T(8,128)S(1)}, f32[128,256]{1,0:T(8,128)S(1)}, f32[8,128]{1,0:T(8,128)S(1)}) custom-call(s32[30]{0:T(128)S(1)} %stack.121.meta, s32[8,128]{1,0:T(8,128)S(1)} %get-tuple-element.53.cols, f32[128,128]{1,0:T(8,128)S(1)} %fusion.live, bf16[128,128,256]{2,1,0:T(8,128)(2,1)S(1)} %bitcast.47, bf16[128,128,256]{2,1,0:T(8,128)(2,1)S(1)} %bitcast.56, ...), custom_call_target="tpu_custom_call" | custom-call | flops 1073741824 | bytes 65536 | tf_op jit(solution)/shard_map/pallas_call | solution.py:31
  141.8 2.8 %collective-permute-start.37 = (bf16[128,256]{1,0:T(8,128)(2,1)S(1)}, bf16[128,256]{1,0:T(8,128)(2,1)S(1)}, u32[]{:S(2)}, u32[]{:S(2)}) collective-permute-start(bf16[128,256]{1,0:T(8,128)(2,1)S(1)} %get-tuple-element.91), channel_id=1, source_target_pairs={{0,4},{1,5},{2,6},{3,7},{4,0},{5,1},{6,2},{7,3},{8,12},{9,13},{10,... | collective-permute-start | bytes 196616 | tf_op jit(solution)/shard_map/ppermute | solution.py:463
  149.6 2.8 %collective-permute-start.41 = (f32[24,128]{1,0:T(8,128)S(1)}, f32[24,128]{1,0:T(8,128)S(1)}, u32[]{:S(2)}, u32[]{:S(2)}) collective-permute-start(f32[24,128]{1,0:T(8,128)S(1)} %add.45.own), channel_id=1, source_target_pairs={{0,4},{1,5},{2,6},{3,7},{4,0},{5,1},{6,2},{7,3},{8,12},{9,13},{10,... | collective-permute-start | bytes 36872 | tf_op jit(solution)/shard_map/ppermute | solution.py:463
  158.0 4.3 %all-to-all-start = ((f32[16,24,128]{2,1,0:T(8,128)}), f32[16,24,128]{2,1,0:T(8,128)S(1)}, u32[]{:S(2)}, u32[]{:S(2)}) async-start(f32[16,24,128]{2,1,0:T(8,128)} %bitcast.34), calls=%async_computation | async-start | bytes 393216 | tf_op jit(solution)/shard_map/all_to_all | solution.py:609
  163.7 6.7 %all-to-all-done = f32[16,24,128]{2,1,0:T(8,128)S(1)} async-done(((f32[16,24,128]{2,1,0:T(8,128)}), f32[16,24,128]{2,1,0:T(8,128)S(1)}, u32[]{:S(2)}, u32[]{:S(2)}) %all-to-all-start) | async-done | bytes 196640 | tf_op jit(solution)/shard_map/all_to_all | solution.py:609
  (126 shorter events, 85.5 us)
Async XLA Ops:
  0.6 7.2 %collective-permute-start.4 = (bf16[3,256,256]{2,1,0:T(8,128)(2,1)}, bf16[3,256,256]{2,1,0:T(8,128)(2,1)S(1)}, u32[]{:S(2)}, u32[]{:S(2)}) collective-permute-start(bf16[3,256,256]{2,1,0:T(8,128)(2,1)} %bitcast.65), channel_id=1, source_target_pairs={{1,0},{3,2},{5,4},{7,6},{9,8},{11,10},{13,12},{15,14},{16,17},{18,... | collective-permute-start | bytes 1179656 | tf_op jit(solution)/shard_map/ppermute | solution.py:463
  3.6 7.8 %collective-permute-start.2 = (bf16[144,256]{1,0:T(8,128)(2,1)S(1)}, bf16[144,256]{1,0:T(8,128)(2,1)S(1)}, u32[]{:S(2)}, u32[]{:S(2)}) collective-permute-start(bf16[144,256]{1,0:T(8,128)(2,1)S(1)} %shard_map.94.a0), channel_id=1, source_target_pairs={{0,6},{1,7},{2,4},{3,5},{4,2},{5,3},{6,0},{7,1},{8,14},{9,15},{10,... | collective-permute-start | bytes 221192 | tf_op jit(solution)/shard_map/ppermute | solution.py:463
  6.8 6.6 %collective-permute-start.1 = (bf16[144,256]{1,0:T(8,128)(2,1)S(1)}, bf16[144,256]{1,0:T(8,128)(2,1)S(1)}, u32[]{:S(2)}, u32[]{:S(2)}) collective-permute-start(bf16[144,256]{1,0:T(8,128)(2,1)S(1)} %shard_map.94.a0), channel_id=1, source_target_pairs={{0,4},{1,5},{2,6},{3,7},{4,0},{5,1},{6,2},{7,3},{8,12},{9,13},{10,... | collective-permute-start | bytes 221192 | tf_op jit(solution)/shard_map/ppermute | solution.py:463
  8.9 23.5 %collective-permute-start.7 = (bf16[6,256,256]{2,1,0:T(8,128)(2,1)S(1)}, bf16[6,256,256]{2,1,0:T(8,128)(2,1)S(1)}, u32[]{:S(2)}, u32[]{:S(2)}) collective-permute-start(bf16[6,256,256]{2,1,0:T(8,128)(2,1)S(1)} %pad_maximum_fusion.t0), channel_id=1, source_target_pairs={{6,0},{14,8},{23,17},{31,25},{36,34},{44,42},{53,51},{61,59},{66,6... | collective-permute-start | bytes 2359304 | tf_op jit(solution)/shard_map/ppermute | solution.py:463
  10.2 22.2 %collective-permute-start.6 = (bf16[6,256,256]{2,1,0:T(8,128)(2,1)S(1)}, bf16[6,256,256]{2,1,0:T(8,128)(2,1)S(1)}, u32[]{:S(2)}, u32[]{:S(2)}) collective-permute-start(bf16[6,256,256]{2,1,0:T(8,128)(2,1)S(1)} %pad_maximum_fusion.t0), channel_id=1, source_target_pairs={{4,0},{12,8},{21,17},{29,25},{38,34},{46,42},{55,51},{63,59},{64,6... | collective-permute-start | bytes 2359304 | tf_op jit(solution)/shard_map/ppermute | solution.py:463
  11.5 20.9 %collective-permute-start.5 = (bf16[6,256,256]{2,1,0:T(8,128)(2,1)S(1)}, bf16[6,256,256]{2,1,0:T(8,128)(2,1)S(1)}, u32[]{:S(2)}, u32[]{:S(2)}) collective-permute-start(bf16[6,256,256]{2,1,0:T(8,128)(2,1)S(1)} %pad_maximum_fusion.t0), channel_id=1, source_target_pairs={{2,0},{10,8},{19,17},{27,25},{32,34},{40,42},{49,51},{57,59},{70,6... | collective-permute-start | bytes 2359304 | tf_op jit(solution)/shard_map/ppermute | solution.py:463
  34.4 6.5 %collective-permute-start.8 = (s16[528,256]{1,0:T(8,128)(2,1)S(1)}, s16[528,256]{1,0:T(8,128)(2,1)S(1)}, u32[]{:S(2)}, u32[]{:S(2)}) collective-permute-start(s16[528,256]{1,0:T(8,128)(2,1)S(1)} %get-tuple-element.56), channel_id=1, source_target_pairs={{0,32},{1,9},{2,34},{3,11},{4,36},{5,13},{6,38},{7,15},{8,40},{9,1... | collective-permute-start | bytes 811016 | tf_op jit(solution)/shard_map/ppermute | solution.py:463
  35.4 10.0 %collective-permute-start.9 = (s16[528,256]{1,0:T(8,128)(2,1)S(1)}, s16[528,256]{1,0:T(8,128)(2,1)S(1)}, u32[]{:S(2)}, u32[]{:S(2)}) collective-permute-start(s16[528,256]{1,0:T(8,128)(2,1)S(1)} %get-tuple-element.57), channel_id=1, source_target_pairs={{0,96},{1,25},{2,98},{3,27},{4,100},{5,29},{6,102},{7,31},{8,104},... | collective-permute-start | bytes 811016 | tf_op jit(solution)/shard_map/ppermute | solution.py:463
  38.5 8.0 %collective-permute-start.10 = (s16[528,256]{1,0:T(8,128)(2,1)S(1)}, s16[528,256]{1,0:T(8,128)(2,1)S(1)}, u32[]{:S(2)}, u32[]{:S(2)}) collective-permute-start(s16[528,256]{1,0:T(8,128)(2,1)S(1)} %get-tuple-element.58), channel_id=1, source_target_pairs={{0,64},{1,17},{2,66},{3,19},{4,68},{5,21},{6,70},{7,23},{8,72},{9,... | collective-permute-start | bytes 811016 | tf_op jit(solution)/shard_map/ppermute | solution.py:463
  47.2 8.1 %collective-permute-start.13 = (s16[528,256]{1,0:T(8,128)(2,1)S(1)}, s16[528,256]{1,0:T(8,128)(2,1)S(1)}, u32[]{:S(2)}, u32[]{:S(2)}) collective-permute-start(s16[528,256]{1,0:T(8,128)(2,1)S(1)} %get-tuple-element.60), channel_id=1, source_target_pairs={{0,16},{1,65},{2,18},{3,67},{4,20},{5,69},{6,22},{7,71},{8,24},{9,... | collective-permute-start | bytes 811016 | tf_op jit(solution)/shard_map/ppermute | solution.py:463
  49.4 8.7 %collective-permute-start.12 = (s16[528,256]{1,0:T(8,128)(2,1)S(1)}, s16[528,256]{1,0:T(8,128)(2,1)S(1)}, u32[]{:S(2)}, u32[]{:S(2)}) collective-permute-start(s16[528,256]{1,0:T(8,128)(2,1)S(1)} %get-tuple-element.60), channel_id=1, source_target_pairs={{0,24},{1,97},{2,26},{3,99},{4,28},{5,101},{6,30},{7,103},{8,16},{... | collective-permute-start | bytes 811016 | tf_op jit(solution)/shard_map/ppermute | solution.py:463
  58.7 9.4 %collective-permute-start.16 = (bf16[512,256]{1,0:T(8,128)(2,1)S(1)}, bf16[512,256]{1,0:T(8,128)(2,1)S(1)}, u32[]{:S(2)}, u32[]{:S(2)}) collective-permute-start(bf16[512,256]{1,0:T(8,128)(2,1)S(1)} %get-tuple-element.62.a), channel_id=1, source_target_pairs={{0,96},{1,25},{2,98},{3,27},{4,100},{5,29},{6,102},{7,31},{8,104},... | collective-permute-start | bytes 786440 | tf_op jit(solution)/shard_map/ppermute | solution.py:463
  61.4 7.9 %collective-permute-start.15 = (bf16[512,256]{1,0:T(8,128)(2,1)S(1)}, bf16[512,256]{1,0:T(8,128)(2,1)S(1)}, u32[]{:S(2)}, u32[]{:S(2)}) collective-permute-start(bf16[512,256]{1,0:T(8,128)(2,1)S(1)} %get-tuple-element.62.a), channel_id=1, source_target_pairs={{0,64},{1,17},{2,66},{3,19},{4,68},{5,21},{6,70},{7,23},{8,72},{9,... | collective-permute-start | bytes 786440 | tf_op jit(solution)/shard_map/ppermute | solution.py:463
  61.4 8.7 %collective-permute-start.14 = (bf16[512,256]{1,0:T(8,128)(2,1)S(1)}, bf16[512,256]{1,0:T(8,128)(2,1)S(1)}, u32[]{:S(2)}, u32[]{:S(2)}) collective-permute-start(bf16[512,256]{1,0:T(8,128)(2,1)S(1)} %get-tuple-element.62.a), channel_id=1, source_target_pairs={{0,32},{1,9},{2,34},{3,11},{4,36},{5,13},{6,38},{7,15},{8,40},{9,1... | collective-permute-start | bytes 786440 | tf_op jit(solution)/shard_map/ppermute | solution.py:463
  98.5 6.5 %collective-permute-start.25 = (s16[528,256]{1,0:T(8,128)(2,1)S(1)}, s16[528,256]{1,0:T(8,128)(2,1)S(1)}, u32[]{:S(2)}, u32[]{:S(2)}) collective-permute-start(s16[528,256]{1,0:T(8,128)(2,1)S(1)} %get-tuple-element.74), channel_id=1, source_target_pairs={{0,32},{1,9},{2,34},{3,11},{4,36},{5,13},{6,38},{7,15},{8,40},{9,1... | collective-permute-start | bytes 811016 | tf_op jit(solution)/shard_map/ppermute | solution.py:463
  99.1 8.9 %collective-permute-start.26 = (s16[528,256]{1,0:T(8,128)(2,1)S(1)}, s16[528,256]{1,0:T(8,128)(2,1)S(1)}, u32[]{:S(2)}, u32[]{:S(2)}) collective-permute-start(s16[528,256]{1,0:T(8,128)(2,1)S(1)} %get-tuple-element.75), channel_id=1, source_target_pairs={{0,96},{1,25},{2,98},{3,27},{4,100},{5,29},{6,102},{7,31},{8,104},... | collective-permute-start | bytes 811016 | tf_op jit(solution)/shard_map/ppermute | solution.py:463
  101.1 8.7 %collective-permute-start.27 = (s16[528,256]{1,0:T(8,128)(2,1)S(1)}, s16[528,256]{1,0:T(8,128)(2,1)S(1)}, u32[]{:S(2)}, u32[]{:S(2)}) collective-permute-start(s16[528,256]{1,0:T(8,128)(2,1)S(1)} %get-tuple-element.76), channel_id=1, source_target_pairs={{0,64},{1,17},{2,66},{3,19},{4,68},{5,21},{6,70},{7,23},{8,72},{9,... | collective-permute-start | bytes 811016 | tf_op jit(solution)/shard_map/ppermute | solution.py:463
  110.5 8.1 %collective-permute-start.30 = (s16[528,256]{1,0:T(8,128)(2,1)S(1)}, s16[528,256]{1,0:T(8,128)(2,1)S(1)}, u32[]{:S(2)}, u32[]{:S(2)}) collective-permute-start(s16[528,256]{1,0:T(8,128)(2,1)S(1)} %get-tuple-element.79), channel_id=1, source_target_pairs={{0,16},{1,65},{2,18},{3,67},{4,20},{5,69},{6,22},{7,71},{8,24},{9,... | collective-permute-start | bytes 811016 | tf_op jit(solution)/shard_map/ppermute | solution.py:463
  112.2 9.3 %collective-permute-start.29 = (s16[528,256]{1,0:T(8,128)(2,1)S(1)}, s16[528,256]{1,0:T(8,128)(2,1)S(1)}, u32[]{:S(2)}, u32[]{:S(2)}) collective-permute-start(s16[528,256]{1,0:T(8,128)(2,1)S(1)} %get-tuple-element.79), channel_id=1, source_target_pairs={{0,24},{1,97},{2,26},{3,99},{4,28},{5,101},{6,30},{7,103},{8,16},{... | collective-permute-start | bytes 811016 | tf_op jit(solution)/shard_map/ppermute | solution.py:463
  115.1 6.5 %collective-permute-start.28 = (s16[528,256]{1,0:T(8,128)(2,1)S(1)}, s16[528,256]{1,0:T(8,128)(2,1)S(1)}, u32[]{:S(2)}, u32[]{:S(2)}) collective-permute-start(s16[528,256]{1,0:T(8,128)(2,1)S(1)} %get-tuple-element.79), channel_id=1, source_target_pairs={{0,8},{1,33},{2,10},{3,35},{4,12},{5,37},{6,14},{7,39},{8,0},{9,41... | collective-permute-start | bytes 811016 | tf_op jit(solution)/shard_map/ppermute | solution.py:463
  122.8 10.5 %collective-permute-start.33 = (bf16[512,256]{1,0:T(8,128)(2,1)S(1)}, bf16[512,256]{1,0:T(8,128)(2,1)S(1)}, u32[]{:S(2)}, u32[]{:S(2)}) collective-permute-start(bf16[512,256]{1,0:T(8,128)(2,1)S(1)} %get-tuple-element.82.a), channel_id=1, source_target_pairs={{0,96},{1,25},{2,98},{3,27},{4,100},{5,29},{6,102},{7,31},{8,104},... | collective-permute-start | bytes 786440 | tf_op jit(solution)/shard_map/ppermute | solution.py:463
  124.6 8.6 %collective-permute-start.32 = (bf16[512,256]{1,0:T(8,128)(2,1)S(1)}, bf16[512,256]{1,0:T(8,128)(2,1)S(1)}, u32[]{:S(2)}, u32[]{:S(2)}) collective-permute-start(bf16[512,256]{1,0:T(8,128)(2,1)S(1)} %get-tuple-element.82.a), channel_id=1, source_target_pairs={{0,64},{1,17},{2,66},{3,19},{4,68},{5,21},{6,70},{7,23},{8,72},{9,... | collective-permute-start | bytes 786440 | tf_op jit(solution)/shard_map/ppermute | solution.py:463
  125.4 8.7 %collective-permute-start.31 = (bf16[512,256]{1,0:T(8,128)(2,1)S(1)}, bf16[512,256]{1,0:T(8,128)(2,1)S(1)}, u32[]{:S(2)}, u32[]{:S(2)}) collective-permute-start(bf16[512,256]{1,0:T(8,128)(2,1)S(1)} %get-tuple-element.82.a), channel_id=1, source_target_pairs={{0,32},{1,9},{2,34},{3,11},{4,36},{5,13},{6,38},{7,15},{8,40},{9,1... | collective-permute-start | bytes 786440 | tf_op jit(solution)/shard_map/ppermute | solution.py:463
  158.0 12.4 %all-to-all-start = ((f32[16,24,128]{2,1,0:T(8,128)}), f32[16,24,128]{2,1,0:T(8,128)S(1)}, u32[]{:S(2)}, u32[]{:S(2)}) async-start(f32[16,24,128]{2,1,0:T(8,128)} %bitcast.34), calls=%async_computation | async-start | bytes 393216 | tf_op jit(solution)/shard_map/all_to_all | solution.py:609
  (36 other events, 332.4 us)
